TPU v7x, 768 devices: a whole 4x8x12 slice. The times are simulated.
768 devices in a mesh: sub: 192 (over y, z, core), own: 4 (over x).
Axes of the slice: x: 4, y: 8, z: 12, core: 2. Of those that a mesh axis runs over, the one named last changes fastest.
Arguments:
- zbasis: bfloat16 [192, 4, 8192, 128], P('sub', 'own'), may hold values from -0.09375 to 0.09375
- stiff: bfloat16 [192, 4, 128, 64, 64], P('sub', 'own')
- ov_index: int32 [192, 4, 2, 512], P('sub', 'own'), may hold values from 0 to 8191
- owner_map: int32 [192, 4, 16, 1], P('sub', 'own'), may hold values from 0 to 3; in each aligned block of 16 rows (0 to 15, 16 to 31, ..., all dimensions but the last counted through in order) at most 8 rows name the same one
- coarse_vec: float32 [192, 4, 128], P('sub', 'own'), may hold values from -6 to 6
Outputs:
- owner_tiles: float32 [192, 4, 4, 8, 8, 384], P('sub', 'own')
- coarse_product: float32 [192, 4, 128], P('sub', 'own')
Inputs may be any that keep to these rules, and one draw needn't show every extreme that they name: `owner_map`: among the 16 tiles of one subdomain no owner is named more than 8 times, and some subdomain names some owner exactly 8 times. `ov_index`: each entry is a row of the subdomain's 8192 unknowns; entries may repeat.
All inputs are finite; a program needn't handle non-finite values.
Results may differ from a plain program's by a relative error of at most 0.00044.
Values may be sent and summed in bfloat16 or wider, within the bound.
No kernel may reach another device: no remote copies, remote signals or barrier semaphores. Data moves between devices by JAX's collectives and lax.ppermute only.
A program may use at most 32 MiB of HBM per device.

v0:
```python
import jax
import jax.numpy as jnp
from jax import lax
from jax.sharding import PartitionSpec as P

TR = 8
SCAP = 8


def with_halo(x, sides, width):
    for axis, dim in sides:
        size, length = (lax.axis_size(axis), x.shape[dim])
        up = [(i, (i + 1) % size) for i in range(size - 1)]
        down = [(j, i) for i, j in up]
        last = lax.slice_in_dim(x, length - width, length, axis=dim)
        first = lax.slice_in_dim(x, 0, width, axis=dim)
        before = lax.ppermute(last, axis, up)
        after = lax.ppermute(first, axis, down)
        x = jnp.concatenate([before, x, after], axis=dim)
    return x


def select_slots(mapping, target, capacity):
    matches = (mapping == target).astype(jnp.int32)
    position = jnp.cumsum(matches, axis=-1) - 1
    slot_ids = jnp.arange(capacity, dtype=jnp.int32)
    chosen = (matches[..., None, :] == 1) & (position[..., None, :] == slot_ids[:, None])
    return chosen.astype(jnp.float32)


def per_device(zbasis, stiff, ov_index, owner_map, coarse_vec):
    deflation = zbasis[0, 0]
    blocks = stiff[0, 0]
    count_blocks, block_size = (blocks.shape[0], blocks.shape[1])
    vec_count = deflation.shape[1]
    applied = (
        jnp.einsum(
            "bij,bjk->bik",
            blocks,
            deflation.reshape(count_blocks, block_size, vec_count),
            preferred_element_type=jnp.float32,
        )
        .reshape(-1, vec_count)
        .astype(jnp.bfloat16)
    )
    margin = ov_index[0, 0]
    margin_len = margin.shape[1]
    edge_rows = jnp.concatenate(
        [jnp.take(applied, margin[0], axis=0), jnp.take(applied, margin[1], axis=0)], axis=0
    )
    extended = with_halo(edge_rows, (("sub", 0),), margin_len)
    from_left = extended[:margin_len]
    from_right = extended[3 * margin_len :]
    self_block = jnp.einsum("na,nb->ab", deflation, applied, preferred_element_type=jnp.float32)
    z_first = jnp.take(deflation, margin[0], axis=0)
    z_second = jnp.take(deflation, margin[1], axis=0)
    left_block = jnp.einsum("na,nb->ab", z_first, from_left, preferred_element_type=jnp.float32)
    right_block = jnp.einsum("na,nb->ab", z_second, from_right, preferred_element_type=jnp.float32)
    neighbours = with_halo(coarse_vec[0], (("sub", 0),), 1)
    highest = lax.Precision.HIGHEST
    coarse_product = (
        jnp.dot(left_block, neighbours[0], precision=highest)
        + jnp.dot(self_block, neighbours[1], precision=highest)
        + jnp.dot(right_block, neighbours[2], precision=highest)
    )
    block_row = jnp.concatenate([left_block, self_block, right_block], axis=1)
    row_tiles = block_row.reshape(-1, TR, 3 * vec_count)
    tile_count = row_tiles.shape[0]
    owners = lax.axis_size("own")
    mapping = owner_map[0, 0, :, 0]
    all_tiles, all_maps = (
        lax.all_gather(row_tiles, "own", axis=0, tiled=True),
        lax.all_gather(mapping.reshape(1, tile_count), "own", axis=0, tiled=True),
    )
    owner_self = lax.axis_index("own")
    chosen = select_slots(all_maps, owner_self, SCAP)
    received = jnp.einsum(
        "pst,ptrc->psrc",
        chosen,
        all_tiles.reshape(owners, tile_count, TR, 3 * vec_count),
        precision=highest,
    )
    return (received[None, None], coarse_product[None, None])


def solution(mesh):
    in_specs = (
        P("sub", "own", None, None),
        P("sub", "own", None, None, None),
        P("sub", "own", None, None),
        P("sub", "own", None, None),
        P("sub", "own", None),
    )
    out_specs = (P("sub", "own", None, None, None, None), P("sub", "own", None))
    return jax.shard_map(
        per_device, mesh=mesh, in_specs=in_specs, out_specs=out_specs, check_vma=False
    )
```

profile of v0, /device:TPU:56, one launch (start us, length us, event | category | flops | bytes accessed | tf_op | source)
XLA Modules:
  0.0 71.9 jit_solution(599122652489369832)
XLA Ops:
  0.6 0.0 copy-start
  0.6 14.9 %collective-permute-start.3 = (f32[1,128]{1,0:T(1,128)}, f32[1,128]{1,0:T(1,128)S(1)}, u32[]{:S(2)}, u32[]{:S(2)}) collective-permute-start(f32[1,128]{1,0:T(1,128)} %bitcast.71), channel_id=1, source_target_pairs={{4,0},{8,4},{12,8},{16,12},{20,16},{24,20},{28,24},{32,28},{36,32}... | collective-permute-start | bytes 1544 | tf_op jit(solution)/shard_map/ppermute | solution.py:18
  15.6 1.9 %collective-permute-start.2 = (f32[1,128]{1,0:T(1,128)}, f32[1,128]{1,0:T(1,128)S(1)}, u32[]{:S(2)}, u32[]{:S(2)}) collective-permute-start(f32[1,128]{1,0:T(1,128)} %bitcast.72), channel_id=1, source_target_pairs={{0,4},{4,8},{8,12},{12,16},{16,20},{20,24},{24,28},{28,32},{32,36}... | collective-permute-start | bytes 1544 | tf_op jit(solution)/shard_map/ppermute | solution.py:17
  17.5 0.8 %fusion.23 = (s32[1,1,1,512]{3,2,1,0:T(1,128)S(1)}, s32[1,1,1,512]{3,2,1,0:T(1,128)S(1)}) fusion(s32[1,1,2,512]{3,2,1,0:T(2,128)} %param.9), kind=kLoop, calls=%fused_computation.45 | loop fusion | bytes 8192 | tf_op jit(solution)/shard_map/slice | solution.py:49
  18.3 4.7 %copy.13 = bf16[128,64,64]{2,1,0:T(8,128)(2,1)} copy(bf16[128,64,64]{0,2,1:T(8,128)(2,1)} %bitcast.63) | data formatting | bytes 2097152 | tf_op jit(solution)/shard_map/squeeze | solution.py:33
  23.1 0.0 copy-done
  23.1 3.6 %convolution_convert_fusion = bf16[128,64,128]{2,1,0:T(8,128)(2,1)} fusion(bf16[128,64,64]{2,1,0:T(8,128)(2,1)} %copy.13, bf16[128,64,128]{2,1,0:T(8,128)(2,1)S(1)} %bitcast.56), kind=kOutput, calls=%fused_computation.4 | convolution fusion | flops 135266304 | bytes 5242880 | tf_op jit(solution)/shard_map/bij,bjk->bik/dot_general | solution.py:37
  26.6 2.9 %gather_fusion.3 = bf16[512,128]{1,0:T(8,128)(2,1)S(1)} fusion(bf16[8192,128]{1,0:T(8,128)(2,1)} %bitcast.59, s32[1024]{0:T(1024)S(1)} %pad_clamp_fusion.1), kind=kCustom, calls=%fused_computation.3.clone | custom fusion | bytes 264192 | tf_op jit(solution)/shard_map/jit(_take)/gather | solution.py:49
  29.6 0.1 broadcast_select_fusion.1
  29.7 5.8 %collective-permute-start.1 = (bf16[512,128]{1,0:T(8,128)(2,1)S(1)}, bf16[512,128]{1,0:T(8,128)(2,1)S(1)}, u32[]{:S(2)}, u32[]{:S(2)}) collective-permute-start(bf16[512,128]{1,0:T(8,128)(2,1)S(1)} %broadcast_select_fusion.1), channel_id=1, source_target_pairs={{4,0},{8,4},{12,8},{16,12},{20,16},{24,20},{28,24},{32,28},{36,32}... | collective-permute-start | bytes 393224 | tf_op jit(solution)/shard_map/ppermute | solution.py:18
  35.5 2.9 %gather_fusion.1 = bf16[512,128]{1,0:T(8,128)(2,1)S(1)} fusion(bf16[8192,128]{1,0:T(8,128)(2,1)} %bitcast.60, s32[1024]{0:T(1024)S(1)} %pad_clamp_fusion), kind=kCustom, calls=%fused_computation.1.clone | custom fusion | bytes 264192 | tf_op jit(solution)/shard_map/jit(_take)/gather | solution.py:49
  38.4 0.1 broadcast_select_fusion
  38.6 0.0 copy-start.2
  38.6 1.9 %collective-permute-start = (bf16[512,128]{1,0:T(8,128)(2,1)S(1)}, bf16[512,128]{1,0:T(8,128)(2,1)S(1)}, u32[]{:S(2)}, u32[]{:S(2)}) collective-permute-start(bf16[512,128]{1,0:T(8,128)(2,1)S(1)} %broadcast_select_fusion), channel_id=1, source_target_pairs={{0,4},{4,8},{8,12},{12,16},{16,20},{20,24},{24,28},{28,32},{32,36}... | collective-permute-start | bytes 393224 | tf_op jit(solution)/shard_map/ppermute | solution.py:17
  40.5 2.3 %convolution_bitcast_fusion.1 = f32[128,128]{0,1:T(8,128)S(1)} fusion(bf16[8192,128]{1,0:T(8,128)(2,1)} %bitcast.61, bf16[1,1,8192,128]{3,2,1,0:T(8,128)(2,1)S(1)} %copy-done), kind=kOutput, calls=%fused_computation.6 | convolution fusion | flops 268435456 | bytes 4259840 | tf_op jit(solution)/shard_map/na,nb->ab/dot_general | solution.py:54
  42.9 0.0 copy-start.1
  42.9 0.0 copy-done.2
  42.9 9.7 %all-gather = s32[4,1,16,1]{2,3,1,0:T(1,128)S(1)} all-gather(s32[1,1,16,1]{2,3,1,0:T(1,128)S(1)} %copy-done.2), channel_id=2, replica_groups=mesh['sub'=192,'own'=4] {'own'}, dimensions={0}, use_global_device_ids=true | all-gather | bytes 320 | tf_op jit(solution)/shard_map/all_gather | solution.py:73
  52.6 0.2 reduce_window_sum.11
  52.8 1.3 %gather_fusion.2 = bf16[512,128]{1,0:T(8,128)(2,1)S(1)} fusion(bf16[8192,128]{1,0:T(8,128)(2,1)S(1)} %bitcast.58, s32[1024]{0:T(1024)S(1)} %pad_clamp_fusion), kind=kCustom, calls=%fused_computation.2.clone | custom fusion | bytes 264192 | tf_op jit(solution)/shard_map/jit(_take)/gather | solution.py:56
  54.1 1.3 %gather_fusion = bf16[512,128]{1,0:T(8,128)(2,1)S(1)} fusion(bf16[8192,128]{1,0:T(8,128)(2,1)S(1)} %bitcast.57, s32[1024]{0:T(1024)S(1)} %pad_clamp_fusion.1), kind=kCustom, calls=%fused_computation.clone | custom fusion | bytes 264192 | tf_op jit(solution)/shard_map/jit(_take)/gather | solution.py:55
  55.5 0.0 copy-done.1
  55.5 0.2 convolution_bitcast_fusion.3
  55.6 0.0 collective-permute-done.1
  55.6 0.3 fusion.4
  56.0 0.0 collective-permute-done
  56.0 0.3 fusion.6
  56.3 0.1 copy.14
  56.4 13.3 %all_gather.7 = f32[64,8,384]{2,1,0:T(8,128)S(1)} all-gather(f32[16,8,384]{2,1,0:T(8,128)S(1)} %bitcast.64), channel_id=1, replica_groups=mesh['sub'=192,'own'=4] {'own'}, dimensions={0}, use_global_device_ids=true | all-gather | bytes 983040 | tf_op jit(solution)/shard_map/all_gather | solution.py:72
  69.8 0.5 convolution_bitcast_fusion
  70.2 0.0 collective-permute-done.3
  70.2 0.2 convolution_bitcast_fusion.2
  70.4 0.8 %copy.16 = f32[1,1,4,8,8,384]{5,4,3,2,1,0:T(8,128)} copy(f32[1,1,4,8,8,384]{5,3,4,2,1,0:T(8,128)S(1)} %convolution_bitcast_fusion) | data formatting | bytes 786432
  71.2 0.0 collective-permute-done.2
  71.2 0.7 fusion.2
  (10 shorter events, 0.1 us)
Async XLA Ops:
  0.6 22.4 %copy-start = (bf16[1,1,8192,128]{3,2,1,0:T(8,128)(2,1)S(1)}, bf16[1,1,8192,128]{3,2,1,0:T(8,128)(2,1)}, u32[]{:S(2)}) copy-start(bf16[1,1,8192,128]{3,2,1,0:T(8,128)(2,1)} %param.7) | copy-start | bytes 6291460
  0.6 69.6 %collective-permute-start.3 = (f32[1,128]{1,0:T(1,128)}, f32[1,128]{1,0:T(1,128)S(1)}, u32[]{:S(2)}, u32[]{:S(2)}) collective-permute-start(f32[1,128]{1,0:T(1,128)} %bitcast.71), channel_id=1, source_target_pairs={{4,0},{8,4},{12,8},{16,12},{20,16},{24,20},{28,24},{32,28},{36,32}... | collective-permute-start | bytes 1544 | tf_op jit(solution)/shard_map/ppermute | solution.py:18
  15.6 55.6 %collective-permute-start.2 = (f32[1,128]{1,0:T(1,128)}, f32[1,128]{1,0:T(1,128)S(1)}, u32[]{:S(2)}, u32[]{:S(2)}) collective-permute-start(f32[1,128]{1,0:T(1,128)} %bitcast.72), channel_id=1, source_target_pairs={{0,4},{4,8},{8,12},{12,16},{16,20},{20,24},{24,28},{28,32},{32,36}... | collective-permute-start | bytes 1544 | tf_op jit(solution)/shard_map/ppermute | solution.py:17
  29.7 25.9 %collective-permute-start.1 = (bf16[512,128]{1,0:T(8,128)(2,1)S(1)}, bf16[512,128]{1,0:T(8,128)(2,1)S(1)}, u32[]{:S(2)}, u32[]{:S(2)}) collective-permute-start(bf16[512,128]{1,0:T(8,128)(2,1)S(1)} %broadcast_select_fusion.1), channel_id=1, source_target_pairs={{4,0},{8,4},{12,8},{16,12},{20,16},{24,20},{28,24},{32,28},{36,32}... | collective-permute-start | bytes 393224 | tf_op jit(solution)/shard_map/ppermute | solution.py:18
  38.6 4.3 %copy-start.2 = (s32[1,1,16,1]{2,3,1,0:T(1,128)S(1)}, s32[1,1,16,1]{2,3,1,0:T(1,128)}, u32[]{:S(2)}) copy-start(s32[1,1,16,1]{2,3,1,0:T(1,128)} %param.10) | copy-start | bytes 196
  38.6 17.4 %collective-permute-start = (bf16[512,128]{1,0:T(8,128)(2,1)S(1)}, bf16[512,128]{1,0:T(8,128)(2,1)S(1)}, u32[]{:S(2)}, u32[]{:S(2)}) collective-permute-start(bf16[512,128]{1,0:T(8,128)(2,1)S(1)} %broadcast_select_fusion), channel_id=1, source_target_pairs={{0,4},{4,8},{8,12},{12,16},{16,20},{20,24},{24,28},{28,32},{32,36}... | collective-permute-start | bytes 393224 | tf_op jit(solution)/shard_map/ppermute | solution.py:17
  42.9 12.6 %copy-start.1 = (f32[1,1,128]{2,1,0:T(1,128)S(1)}, f32[1,1,128]{2,1,0:T(1,128)}, u32[]{:S(2)}) copy-start(f32[1,1,128]{2,1,0:T(1,128)} %param.11) | copy-start | bytes 1540
where the time goes:
time: 72.6 us; the launch traced here: 71.9 us
  starting transfers between devices  24.5 us (34%)
  blocking collectives  23 us (32%)
  local copies, waits for them, and re-layouts  15 us (21%)
  matrix products  8.02 us (11%)
  between operations  0.83 us (1%)
    ppermute x2, starting transfers between devices, with_halo(): after = lax.ppermute(first, axis, down)  20.7 us
    all_gather x1, blocking collectives, per_device(): lax.all_gather(row_tiles, 'own', axis=0, tiled=True)  13.3 us
    all_gather x1, blocking collectives, per_device(): lax.all_gather(mapping.reshape(1, tile_count), 'own', axis=0, tiled=True)  9.67 us
    squeeze x1, local copies, waits for them, and re-layouts, per_device(): blocks = stiff[0, 0]  4.74 us
    ppermute x2, starting transfers between devices, with_halo(): before = lax.ppermute(last, axis, up)  3.84 us
    dot_general x1, matrix products, per_device(): jnp.einsum('bij,bjk->bik', blocks, deflation.reshape(count_blocks, block_...  3.59 us
    gather x1, local copies, waits for them, and re-layouts, per_device(): jnp.take(applied, margin[1], axis=0)  2.91 us
    gather x1, local copies, waits for them, and re-layouts, per_device(): jnp.take(applied, margin[0], axis=0)  2.91 us
  transfers between devices with their start and end apart: 4, of which 0 were waited for; matrix products, arithmetic and copies ran while one was open for 32% of the time, Pallas kernels for 0%

commit v1 on v0

v1 whole, which is shorter than its diff:
```python
import functools

import jax
import jax.numpy as jnp
from jax import lax
from jax.experimental import pallas as pl
from jax.experimental.pallas import tpu as pltpu
from jax.sharding import PartitionSpec as P

TR = 8
SCAP = 8
PAD = 16
UNROLL = 8
F32 = jnp.float32
BF16 = jnp.bfloat16
SMEM = pl.BlockSpec(memory_space=pltpu.SMEM)
VMEM = pl.BlockSpec(memory_space=pltpu.VMEM)
ANY = pl.BlockSpec(memory_space=pl.ANY)


def parity():
    return lax.rem(lax.axis_index("sub"), 2)


def split3(x):
    hi = x.astype(BF16)
    rest = x - hi.astype(F32)
    mid = rest.astype(BF16)
    low = (rest - mid.astype(F32)).astype(BF16)
    return jnp.concatenate([hi, mid, low, jnp.zeros((PAD - 3, x.shape[1]), BF16)], axis=0)


def gather_rows(idx, side, source, target, base, count):
    @pl.loop(0, count // UNROLL)
    def _(g):
        first = g * UNROLL
        for r in range(UNROLL):
            row = idx[side, first + r]
            target[pl.ds(base + first + r, 1), :] = source[pl.ds(row, 1), :]


def apply_kernel(idx, z_hbm, a_hbm, vec, cross, inner, applied, z_v, a_v, x_v, w_v, rows_v, sems):
    order, _, nb = a_v.shape
    half = order // 2
    lanes = z_v.shape[1]
    count = idx.shape[1]
    pitch = nb + 8
    copy_a = pltpu.make_async_copy(a_hbm, a_v, sems.at[0])
    copy_z = pltpu.make_async_copy(z_hbm, z_v, sems.at[1])
    copy_a.start()
    copy_z.start()
    extra = split3(vec[...])
    cross[pl.ds(count, PAD), :] = extra
    inner[pl.ds(count, PAD), :] = extra
    copy_a.wait()

    @pl.loop(0, half, unroll=4)
    def _(p):
        pair = jnp.concatenate([a_v[p], a_v[p + half]], axis=0)
        x_v[pl.ds(pl.multiple_of(p * pitch, 8), nb), :] = pair.T.astype(F32)

    copy_z.wait()

    @pl.loop(0, nb, unroll=8)
    def _(b):
        at = pl.multiple_of(b * order, order)
        left = x_v[pl.ds(b, half, stride=pitch), :].astype(BF16)
        zb = z_v[pl.ds(at, order), :]
        zero = jnp.zeros_like(zb)
        right = jnp.concatenate(
            [jnp.concatenate([zb, zero], axis=1), jnp.concatenate([zero, zb], axis=1)], axis=0
        )
        out = jnp.dot(left, right, preferred_element_type=F32)
        out = jnp.concatenate([out[:, :lanes], out[:, lanes:]], axis=0)
        w_v[pl.ds(at, order), :] = out
        applied[pl.ds(at, order), :] = out.astype(BF16)

    mine = parity()
    gather_rows(idx, mine, w_v, rows_v, 0, count)
    cross[pl.ds(0, count), :] = rows_v[pl.ds(0, count), :].astype(BF16)
    gather_rows(idx, 1 - mine, w_v, rows_v, count, count)
    inner[pl.ds(0, count), :] = rows_v[pl.ds(count, count), :].astype(BF16)


def local_kernel(idx, z, applied, self_block, zt, z_f, rows_v):
    n, lanes = z.shape
    count = idx.shape[1]
    step = 512

    self_block[...] = jnp.zeros_like(self_block)

    @pl.loop(0, n // step)
    def _(s):
        at = pl.multiple_of(s * step, step)
        part = z[pl.ds(at, step), :]
        z_f[pl.ds(at, step), :] = part.astype(F32)
        self_block[...] += lax.dot_general(
            part, applied[pl.ds(at, step), :], (((0,), (0,)), ((), ())), preferred_element_type=F32
        )

    mine = parity()
    gather_rows(idx, mine, z_f, rows_v, 0, count)
    gather_rows(idx, 1 - mine, z_f, rows_v, count, count)
    zt[...] = rows_v[...].astype(BF16).T


def pack_kernel(owner, cross, inner, zt, self_block, vec, tiles, product, row_v, used):
    lanes = self_block.shape[0]
    count = zt.shape[1] // 2
    mine = parity()

    def joined(ref):
        extra = ref[pl.ds(count, PAD), :].astype(F32)
        return extra[0:1] + (extra[1:2] + extra[2:3])

    tiles[...] = jnp.zeros_like(tiles)
    by_cross = jnp.dot(zt[:, :count], cross[pl.ds(0, count), :], preferred_element_type=F32)
    by_inner = jnp.dot(zt[:, count:], inner[pl.ds(0, count), :], preferred_element_type=F32)
    own = self_block[...]
    at = pl.multiple_of(mine * (2 * lanes), lanes)
    row_v[:, pl.ds(at, lanes)] = by_cross
    row_v[:, pl.ds(pl.multiple_of(2 * lanes - at, lanes), lanes)] = by_inner
    row_v[:, pl.ds(lanes, lanes)] = own
    total = by_cross * joined(cross) + own * vec[...] + by_inner * joined(inner)
    product[...] = jnp.sum(total.T, axis=0, keepdims=True)
    for q in range(tiles.shape[0]):
        used[q] = 0
    for t in range(owner.shape[1]):
        q = owner[0, t]
        slot = used[q]
        used[q] = slot + 1
        tiles[q, slot] = row_v[pl.ds(t * TR, TR), :]


def per_device(zbasis, stiff, ov_index, owner_map, coarse_vec):
    z = zbasis[0, 0]
    a = jnp.transpose(stiff[0, 0], (1, 2, 0))
    idx = ov_index[0, 0]
    owner = owner_map[0, 0, :, 0].reshape(1, -1)
    vec = coarse_vec[0]
    n, lanes = z.shape
    order, _, nb = a.shape
    count = idx.shape[1]
    chain = lax.axis_size("sub")
    owners = lax.axis_size("own")
    sent = jax.ShapeDtypeStruct((count + PAD, lanes), BF16)
    cross, inner, applied = pl.pallas_call(
        apply_kernel,
        name="apply",
        out_shape=(sent, sent, jax.ShapeDtypeStruct((n, lanes), BF16)),
        in_specs=[SMEM, ANY, ANY, VMEM],
        out_specs=(VMEM, VMEM, VMEM),
        scratch_shapes=[
            pltpu.VMEM((n, lanes), BF16),
            pltpu.VMEM((order, order, nb), BF16),
            pltpu.VMEM((order // 2 * (nb + 8), 2 * order), F32),
            pltpu.VMEM((n, lanes), F32),
            pltpu.VMEM((2 * count, lanes), F32),
            pltpu.SemaphoreType.DMA((2,)),
        ],
        compiler_params=pltpu.CompilerParams(vmem_limit_bytes=40 << 20),
        cost_estimate=pl.CostEstimate(flops=2 * n * order * lanes, bytes_accessed=6 << 20, transcendentals=0),
    )(idx, z, a, vec)
    pairs = [(i, i + 1) for i in range(1, chain - 1, 2)]
    got_cross = lax.ppermute(cross, "sub", pairs + [(j, i) for i, j in pairs])
    got_inner = lax.ppermute(inner, "sub", [(i, i ^ 1) for i in range(chain)])
    self_block, zt = pl.pallas_call(
        local_kernel,
        name="local",
        out_shape=(
            jax.ShapeDtypeStruct((lanes, lanes), F32),
            jax.ShapeDtypeStruct((lanes, 2 * count), BF16),
        ),
        in_specs=[SMEM, VMEM, VMEM],
        out_specs=(VMEM, VMEM),
        scratch_shapes=[pltpu.VMEM((n, lanes), F32), pltpu.VMEM((2 * count, lanes), F32)],
        compiler_params=pltpu.CompilerParams(vmem_limit_bytes=40 << 20),
        cost_estimate=pl.CostEstimate(flops=2 * n * lanes * lanes, bytes_accessed=5 << 20, transcendentals=0),
    )(idx, z, applied)
    tiles, product = pl.pallas_call(
        pack_kernel,
        name="pack",
        out_shape=(
            jax.ShapeDtypeStruct((owners, SCAP, TR, 3 * lanes), F32),
            jax.ShapeDtypeStruct((1, lanes), F32),
        ),
        in_specs=[SMEM, VMEM, VMEM, VMEM, VMEM, VMEM],
        out_specs=(VMEM, VMEM),
        scratch_shapes=[pltpu.VMEM((lanes, 3 * lanes), F32), pltpu.SMEM((owners,), jnp.int32)],
        compiler_params=pltpu.CompilerParams(vmem_limit_bytes=16 << 20),
    )(owner, got_cross, got_inner, zt, self_block, vec)
    received = lax.all_to_all(tiles, "own", 0, 0, tiled=True)
    return received[None, None], product[None]


def solution(mesh):
    in_specs = (
        P("sub", "own", None, None),
        P("sub", "own", None, None, None),
        P("sub", "own", None, None),
        P("sub", "own", None, None),
        P("sub", "own", None),
    )
    out_specs = (P("sub", "own", None, None, None, None), P("sub", "own", None))
    return jax.shard_map(
        per_device, mesh=mesh, in_specs=in_specs, out_specs=out_specs, check_vma=False
    )
```

time: 72.6 us -> 52.5 us (0.72)
  Pallas kernels: 0 us -> 17.1 us
  blocking collectives: 23 us -> 12.8 us
  local copies, waits for them, and re-layouts: 15 us -> 4.9 us
  matrix products: 8.02 us -> 0 us
  starting transfers between devices: 24.5 us -> 16.7 us
    all_gather x2 -> x0, blocking collectives: 23 us -> none  [the longest x1 13.3 us: per_device(): lax.all_gather(row_tiles, 'own', axis=0, tiled=True)]
    pallas_call x0 -> x3, Pallas kernels: none -> 17.1 us  [the longest x1 8.08 us: per_device(): pl.pallas_call(apply_kernel, name='apply', out_shape=(sent, sent, jax.Sha...]
    all_to_all x0 -> x1, blocking collectives: none -> 12.8 us  [per_device(): received = lax.all_to_all(tiles, 'own', 0, 0, tiled=True)]
    gather x4 -> x0, local copies, waits for them, and re-layouts: 8.5 us -> none  [the longest x1 2.91 us: per_device(): jnp.take(applied, margin[1], axis=0)]
    dot_general x8 -> x0, matrix products: 8.02 us -> none  [the longest x1 3.59 us: per_device(): jnp.einsum('bij,bjk->bik', blocks, deflation.reshape(count_blocks, block_...]
    ppermute x4 -> x2, starting transfers between devices: 24.5 us -> 16.7 us  [the longest x1 14.8 us: per_device(): got_cross = lax.ppermute(cross, 'sub', pairs + [(j, i) for i, j in pairs])]
    squeeze x1 -> x0, local copies, waits for them, and re-layouts: 4.74 us -> none  [per_device(): blocks = stiff[0, 0]]
    unnamed x7 -> x11, local copies, waits for them, and re-layouts: 0.86 us -> 4.9 us
  transfers between devices with their start and end apart: 4 -> 2, of which waited for: 0 -> 0; matrix products, arithmetic and copies ran while one was open for 32% -> 0% of each run, Pallas kernels for 0% -> 15%
where the time goes in v1:
time: 52.5 us; the launch traced here: 52.2 us
  Pallas kernels  17.1 us (33%)
  starting transfers between devices  16.7 us (32%)
  blocking collectives  12.8 us (24%)
  local copies, waits for them, and re-layouts  4.9 us (9%)
  between operations  0.7 us (1%)
    ppermute x1, starting transfers between devices, per_device(): got_cross = lax.ppermute(cross, 'sub', pairs + [(j, i) for i, j in pairs])  14.8 us
    all_to_all x1, blocking collectives, per_device(): received = lax.all_to_all(tiles, 'own', 0, 0, tiled=True)  12.8 us
    pallas_call x1, Pallas kernels, per_device(): pl.pallas_call(apply_kernel, name='apply', out_shape=(sent, sent, jax.Sha...  8.08 us
    pallas_call x1, Pallas kernels, per_device(): pl.pallas_call(local_kernel, name='local', out_shape=(jax.ShapeDtypeStruc...  7.63 us
    unnamed x11, local copies, waits for them, and re-layouts  4.9 us
    ppermute x1, starting transfers between devices, per_device(): got_inner = lax.ppermute(inner, 'sub', [(i, i ^ 1) for i in range(chain)])  1.92 us
    pallas_call x1, Pallas kernels, per_device(): pl.pallas_call(pack_kernel, name='pack', out_shape=(jax.ShapeDtypeStruct(...  1.38 us
  transfers between devices with their start and end apart: 2, of which 0 were waited for; matrix products, arithmetic and copies ran while one was open for 0% of the time, Pallas kernels for 15%

profile of v1, /device:TPU:56, one launch (start us, length us, event | category | flops | bytes accessed | tf_op | source)
XLA Modules:
  0.0 52.2 jit_solution(2262874260340851773)
XLA Ops:
  0.6 0.0 copy-start
  0.6 1.6 %copy-done = bf16[1,1,8192,128]{3,2,1,0:T(8,128)(2,1)S(1)} copy-done((bf16[1,1,8192,128]{3,2,1,0:T(8,128)(2,1)S(1)}, bf16[1,1,8192,128]{3,2,1,0:T(8,128)(2,1)}, u32[]{:S(2)}) %copy-start) | copy-done | bytes 2097176
  2.2 0.0 copy-start.1
  2.2 1.2 %copy-done.1 = bf16[1,1,128,64,64]{2,4,3,1,0:T(8,128)(2,1)S(1)} copy-done((bf16[1,1,128,64,64]{2,4,3,1,0:T(8,128)(2,1)S(1)}, bf16[1,1,128,64,64]{2,4,3,1,0:T(8,128)(2,1)}, u32[]{:S(2)}) %copy-start.1) | copy-done | bytes 1048600
  3.4 0.0 copy-start.2
  3.5 0.7 %copy-done.2 = s32[1,1,2,512]{3,2,1,0:T(2,128)S(1)} copy-done((s32[1,1,2,512]{3,2,1,0:T(2,128)S(1)}, s32[1,1,2,512]{3,2,1,0:T(2,128)}, u32[]{:S(2)}) %copy-start.2) | copy-done | bytes 4120
  4.1 0.0 copy-start.3
  4.1 0.7 %copy-done.3 = f32[1,1,128]{2,1,0:T(1,128)S(1)} copy-done((f32[1,1,128]{2,1,0:T(1,128)S(1)}, f32[1,1,128]{2,1,0:T(1,128)}, u32[]{:S(2)}) %copy-start.3) | copy-done | bytes 536
  4.8 8.1 %apply.1 = (bf16[528,128]{1,0:T(8,128)(2,1)S(1)}, bf16[528,128]{1,0:T(8,128)(2,1)S(1)}, bf16[8192,128]{1,0:T(8,128)(2,1)S(1)}) custom-call(s32[2,512]{1,0:T(2,128)S(1)} %bitcast.12, bf16[8192,128]{1,0:T(8,128)(2,1)S(1)} %bitcast.9, bf16[64,64,128]{2,1,0:T(8,128)(2,1)S(1)} %bitcast.11, f32[1,128]{1,0:T(1,128)S(1)} %bitcast.14), custom_call_target="tpu_custom_call" | custom-call | flops 134217728 | bytes 6291456 | tf_op jit(solution)/shard_map/apply/pallas_call | solution.py:147
  12.9 14.8 %collective-permute-start = (bf16[528,128]{1,0:T(8,128)(2,1)S(1)}, bf16[528,128]{1,0:T(8,128)(2,1)S(1)}, u32[]{:S(2)}, u32[]{:S(2)}) collective-permute-start(bf16[528,128]{1,0:T(8,128)(2,1)S(1)} %get-tuple-element.9), channel_id=1, source_target_pairs={{4,8},{12,16},{20,24},{28,32},{36,40},{44,48},{52,56},{60,64},{68,... | collective-permute-start | bytes 405512 | tf_op jit(solution)/shard_map/ppermute | solution.py:165
  27.7 1.9 %collective-permute-start.1 = (bf16[528,128]{1,0:T(8,128)(2,1)S(1)}, bf16[528,128]{1,0:T(8,128)(2,1)S(1)}, u32[]{:S(2)}, u32[]{:S(2)}) collective-permute-start(bf16[528,128]{1,0:T(8,128)(2,1)S(1)} %get-tuple-element.10), channel_id=1, source_target_pairs={{0,4},{4,0},{8,12},{12,8},{16,20},{20,16},{24,28},{28,24},{32,36},... | collective-permute-start | bytes 405512 | tf_op jit(solution)/shard_map/ppermute | solution.py:166
  29.6 0.0 copy-start.4
  29.6 7.6 %local.1 = (f32[128,128]{1,0:T(8,128)S(1)}, bf16[128,1024]{1,0:T(8,128)(2,1)S(1)}) custom-call(s32[2,512]{1,0:T(2,128)S(1)} %bitcast.13, bf16[8192,128]{1,0:T(8,128)(2,1)S(1)} %bitcast.10, bf16[8192,128]{1,0:T(8,128)(2,1)S(1)} %get-tuple-element.11.applied), custom_call_target="tpu_custom_call" | custom-call | flops 268435456 | bytes 5242880 | tf_op jit(solution)/shard_map/local/pallas_call | solution.py:167
  37.3 0.0 collective-permute-done.cross
  37.3 0.0 collective-permute-done.1.inner
  37.3 0.0 copy-done.4
  37.3 1.4 %pack.1 = (f32[4,8,8,384]{3,2,1,0:T(8,128)S(1)}, f32[1,128]{1,0:T(1,128)}) custom-call(s32[1,16]{1,0:T(1,128)S(1)} %bitcast.16, bf16[528,128]{1,0:T(8,128)(2,1)S(1)} %collective-permute-done.cross, bf16[528,128]{1,0:T(8,128)(2,1)S(1)} %collective-permute-done.1.inner, bf16[128,1024]{1,0:T(8,128)(2,1)S(1)} %get-tuple-element.12.zt, ...), custom_call_target="tpu_custom_call" | custom-call | tf_op jit(solution)/shard_map/pack/pallas_call | solution.py:180
  38.7 12.8 %all_to_all.5 = f32[4,8,8,384]{3,2,1,0:T(8,128)S(1)} all-to-all(f32[4,8,8,384]{3,2,1,0:T(8,128)S(1)} %get-tuple-element.14), channel_id=1, replica_groups=mesh['sub'=192,'own'=4] {'own'}, dimensions={0} | all-to-all | bytes 786432 | tf_op jit(solution)/shard_map/all_to_all | solution.py:192
  51.5 0.7 %copy.8 = f32[1,1,4,8,8,384]{5,4,3,2,1,0:T(8,128)} copy(f32[1,1,4,8,8,384]{5,4,3,2,1,0:T(8,128)S(1)} %bitcast.17) | data formatting | bytes 786432
Async XLA Ops:
  0.6 1.6 %copy-start = (bf16[1,1,8192,128]{3,2,1,0:T(8,128)(2,1)S(1)}, bf16[1,1,8192,128]{3,2,1,0:T(8,128)(2,1)}, u32[]{:S(2)}) copy-start(bf16[1,1,8192,128]{3,2,1,0:T(8,128)(2,1)} %param.5) | copy-start | bytes 6291460
  2.2 1.2 %copy-start.1 = (bf16[1,1,128,64,64]{2,4,3,1,0:T(8,128)(2,1)S(1)}, bf16[1,1,128,64,64]{2,4,3,1,0:T(8,128)(2,1)}, u32[]{:S(2)}) copy-start(bf16[1,1,128,64,64]{2,4,3,1,0:T(8,128)(2,1)} %param.6) | copy-start | bytes 3145732
  3.4 0.7 %copy-start.2 = (s32[1,1,2,512]{3,2,1,0:T(2,128)S(1)}, s32[1,1,2,512]{3,2,1,0:T(2,128)}, u32[]{:S(2)}) copy-start(s32[1,1,2,512]{3,2,1,0:T(2,128)} %param.7) | copy-start | bytes 12292
  4.1 0.7 %copy-start.3 = (f32[1,1,128]{2,1,0:T(1,128)S(1)}, f32[1,1,128]{2,1,0:T(1,128)}, u32[]{:S(2)}) copy-start(f32[1,1,128]{2,1,0:T(1,128)} %param.9) | copy-start | bytes 1540
  12.9 24.4 %collective-permute-start = (bf16[528,128]{1,0:T(8,128)(2,1)S(1)}, bf16[528,128]{1,0:T(8,128)(2,1)S(1)}, u32[]{:S(2)}, u32[]{:S(2)}) collective-permute-start(bf16[528,128]{1,0:T(8,128)(2,1)S(1)} %get-tuple-element.9), channel_id=1, source_target_pairs={{4,8},{12,16},{20,24},{28,32},{36,40},{44,48},{52,56},{60,64},{68,... | collective-permute-start | bytes 405512 | tf_op jit(solution)/shard_map/ppermute | solution.py:165
  27.7 9.6 %collective-permute-start.1 = (bf16[528,128]{1,0:T(8,128)(2,1)S(1)}, bf16[528,128]{1,0:T(8,128)(2,1)S(1)}, u32[]{:S(2)}, u32[]{:S(2)}) collective-permute-start(bf16[528,128]{1,0:T(8,128)(2,1)S(1)} %get-tuple-element.10), channel_id=1, source_target_pairs={{0,4},{4,0},{8,12},{12,8},{16,20},{20,16},{24,28},{28,24},{32,36},... | collective-permute-start | bytes 405512 | tf_op jit(solution)/shard_map/ppermute | solution.py:166
  29.6 7.7 %copy-start.4 = (s32[1,1,16,1]{2,3,1,0:T(1,128)S(1)}, s32[1,1,16,1]{2,3,1,0:T(1,128)}, u32[]{:S(2)}) copy-start(s32[1,1,16,1]{2,3,1,0:T(1,128)} %param.8) | copy-start | bytes 196

commit v2 on v1

v2 whole, which is shorter than its diff:
```python
import jax
import jax.numpy as jnp
from jax import lax
from jax.experimental import pallas as pl
from jax.experimental.pallas import tpu as pltpu
from jax.sharding import PartitionSpec as P

TR = 8
SCAP = 8
PAD = 16
STEP = 512
A_CUTS = 2
Z_CUTS = 4
ROOM = 58 << 20
BASIS_ROOM = 40 << 20
PACK_ROOM = 16 << 20
F32 = jnp.float32
BF16 = jnp.bfloat16
SMEM = pl.BlockSpec(memory_space=pltpu.SMEM)
VMEM = pl.BlockSpec(memory_space=pltpu.VMEM)
HBM = pl.BlockSpec(memory_space=pltpu.HBM)


def parity():
    return lax.rem(lax.axis_index("sub"), 2)


def split3(x):
    hi = x.astype(BF16)
    rest = x - hi.astype(F32)
    mid = rest.astype(BF16)
    low = (rest - mid.astype(F32)).astype(BF16)
    return jnp.concatenate([hi, mid, low, jnp.zeros((PAD - 3, x.shape[1]), BF16)], axis=0)


def gather_rows(idx, side, source, target):
    for r in range(idx.shape[1]):
        target[pl.ds(r, 1), :] = source[pl.ds(idx[side, r], 1), :]


def apply_kernel(
    idx_hbm, z_hbm, a_hbm, vec, cross, inner, self_block, idx, z_v, a_v, x_v, w_v, rows_v, sent, self_v, sems
):
    order, _, nb = a_v.shape
    half = order // 2
    n, lanes = z_v.shape
    count = idx.shape[1]
    pitch = nb + 8
    quarter = half // A_CUTS
    slab = n // Z_CUTS
    copy_idx = pltpu.make_async_copy(idx_hbm, idx, sems.at[0])
    copy_idx.start()
    copies_a, copies_z = [], []
    for c in range(A_CUTS):
        for h in range(2):
            part = pl.ds(h * half + c * quarter, quarter)
            copies_a.append(
                pltpu.make_async_copy(a_hbm.at[part], a_v.at[part], sems.at[1 + 2 * c + h])
            )
            copies_a[-1].start()
    for c in range(Z_CUTS):
        part = pl.ds(c * slab, slab)
        copies_z.append(
            pltpu.make_async_copy(z_hbm.at[part], z_v.at[part], sems.at[1 + 2 * A_CUTS + c])
        )
        copies_z[-1].start()
    extra = split3(vec[...])
    for side in range(2):
        sent[side, pl.ds(count, PAD), :] = extra
    for c in range(A_CUTS):
        copies_a[2 * c].wait()
        copies_a[2 * c + 1].wait()
        for p in range(c * quarter, (c + 1) * quarter):
            pair = jnp.concatenate([a_v[p], a_v[p + half]], axis=0)
            x_v[pl.ds(p * pitch, nb), :] = pair.T.astype(F32)
    copy_idx.wait()
    for b in range(nb):
        if b * order % slab == 0:
            copies_z[b * order // slab].wait()
        at = b * order
        left = x_v[pl.ds(b, half, stride=pitch), :].astype(BF16)
        zb = z_v[pl.ds(at, order), :]
        zero = jnp.zeros_like(zb)
        right = jnp.concatenate(
            [jnp.concatenate([zb, zero], axis=1), jnp.concatenate([zero, zb], axis=1)], axis=0
        )
        out = jnp.dot(left, right, preferred_element_type=F32)
        w_v[pl.ds(at, order), :] = jnp.concatenate([out[:, :lanes], out[:, lanes:]], axis=0)
    mine = parity()
    leaving = []
    for slot, target in enumerate((cross, inner)):
        rows = rows_v.at[pl.ds(slot * count, count)]
        gather_rows(idx, mine if slot == 0 else 1 - mine, w_v, rows)
        sent[slot, pl.ds(0, count), :] = rows[...].astype(BF16)
        leaving.append(pltpu.make_async_copy(sent.at[slot], target, sems.at[slot]))
        leaving[-1].start()
    total = jnp.zeros((lanes, lanes), F32)
    for at in range(0, n, STEP):
        total += lax.dot_general(
            z_v[pl.ds(at, STEP), :],
            w_v[pl.ds(at, STEP), :].astype(BF16),
            (((0,), (0,)), ((), ())),
            preferred_element_type=F32,
        )
    self_v[...] = total
    leaving.append(pltpu.make_async_copy(self_v, self_block, sems.at[2]))
    leaving[-1].start()
    for copy in leaving:
        copy.wait()


def basis_kernel(idx, z, zt, z_f, rows_v):
    count = idx.shape[1]
    mine = parity()
    for at in range(0, z.shape[0], STEP):
        z_f[pl.ds(at, STEP), :] = z[pl.ds(at, STEP), :].astype(F32)
    for slot in range(2):
        rows = rows_v.at[pl.ds(slot * count, count)]
        gather_rows(idx, mine if slot == 0 else 1 - mine, z_f, rows)
    zt[...] = rows_v[...].astype(BF16).T


def pack_kernel(owner, cross, inner, zt, self_block, vec, tiles, product, row_v, used):
    lanes = self_block.shape[0]
    count = zt.shape[1] // 2
    mine = parity()

    def joined(ref):
        extra = ref[pl.ds(count, PAD), :].astype(F32)
        return extra[0:1] + (extra[1:2] + extra[2:3])

    tiles[...] = jnp.zeros_like(tiles)
    by_cross = jnp.dot(zt[:, :count], cross[pl.ds(0, count), :], preferred_element_type=F32)
    by_inner = jnp.dot(zt[:, count:], inner[pl.ds(0, count), :], preferred_element_type=F32)
    own = self_block[...]
    at = pl.multiple_of(mine * (2 * lanes), lanes)
    row_v[:, pl.ds(at, lanes)] = by_cross
    row_v[:, pl.ds(pl.multiple_of(2 * lanes - at, lanes), lanes)] = by_inner
    row_v[:, pl.ds(lanes, lanes)] = own
    total = by_cross * joined(cross) + own * vec[...] + by_inner * joined(inner)
    product[...] = jnp.sum(total.T, axis=0, keepdims=True)
    for q in range(tiles.shape[0]):
        used[q] = 0
    for t in range(owner.shape[1]):
        q = owner[0, t]
        slot = used[q]
        used[q] = slot + 1
        tiles[q, slot] = row_v[pl.ds(t * TR, TR), :]


def per_device(zbasis, stiff, ov_index, owner_map, coarse_vec):
    z = zbasis[0, 0]
    a = jnp.transpose(stiff[0, 0], (1, 2, 0))
    idx = ov_index[0, 0]
    owner = owner_map[0, 0, :, 0].reshape(1, -1)
    vec = coarse_vec[0]
    n, lanes = z.shape
    order, _, nb = a.shape
    count = idx.shape[1]
    chain = lax.axis_size("sub")
    owners = lax.axis_size("own")
    sent = jax.ShapeDtypeStruct((count + PAD, lanes), BF16)
    square = jax.ShapeDtypeStruct((lanes, lanes), F32)
    basis = jax.ShapeDtypeStruct((lanes, 2 * count), BF16)
    cross, inner, self_block = pl.pallas_call(
        apply_kernel,
        name="apply",
        out_shape=(sent, sent, square),
        in_specs=[HBM, HBM, HBM, VMEM],
        out_specs=(HBM, HBM, HBM),
        scratch_shapes=[
            pltpu.SMEM((2, count), jnp.int32),
            pltpu.VMEM((n, lanes), BF16),
            pltpu.VMEM((order, order, nb), BF16),
            pltpu.VMEM((order // 2 * (nb + 8), 2 * order), F32),
            pltpu.VMEM((n, lanes), F32),
            pltpu.VMEM((2 * count, lanes), F32),
            pltpu.VMEM((2, count + PAD, lanes), BF16),
            pltpu.VMEM((lanes, lanes), F32),
            pltpu.SemaphoreType.DMA((1 + 2 * A_CUTS + Z_CUTS,)),
        ],
        compiler_params=pltpu.CompilerParams(vmem_limit_bytes=ROOM),
        cost_estimate=pl.CostEstimate(flops=1 << 29, bytes_accessed=4 << 20, transcendentals=0),
    )(idx, z, a, vec)
    pairs = [(i, i + 1) for i in range(1, chain - 1, 2)]
    got_cross = lax.ppermute(cross, "sub", pairs + [(j, i) for i, j in pairs])
    got_inner = lax.ppermute(inner, "sub", [(i, i ^ 1) for i in range(chain)])
    zt = pl.pallas_call(
        basis_kernel,
        name="basis",
        out_shape=basis,
        in_specs=[SMEM, VMEM],
        out_specs=VMEM,
        scratch_shapes=[pltpu.VMEM((n, lanes), F32), pltpu.VMEM((2 * count, lanes), F32)],
        compiler_params=pltpu.CompilerParams(vmem_limit_bytes=BASIS_ROOM),
        cost_estimate=pl.CostEstimate(flops=1 << 28, bytes_accessed=2 << 20, transcendentals=0),
    )(idx, z)
    tiles, product = pl.pallas_call(
        pack_kernel,
        name="pack",
        out_shape=(
            jax.ShapeDtypeStruct((owners, SCAP, TR, 3 * lanes), F32),
            jax.ShapeDtypeStruct((1, lanes), F32),
        ),
        in_specs=[SMEM, VMEM, VMEM, VMEM, VMEM, VMEM],
        out_specs=(VMEM, VMEM),
        scratch_shapes=[pltpu.VMEM((lanes, 3 * lanes), F32), pltpu.SMEM((owners,), jnp.int32)],
        compiler_params=pltpu.CompilerParams(vmem_limit_bytes=PACK_ROOM),
    )(owner, got_cross, got_inner, zt, self_block, vec)
    received = lax.all_to_all(tiles, "own", 0, 0, tiled=True)
    return received[None, None], product[None]


def solution(mesh):
    in_specs = (
        P("sub", "own", None, None),
        P("sub", "own", None, None, None),
        P("sub", "own", None, None),
        P("sub", "own", None, None),
        P("sub", "own", None),
    )
    out_specs = (P("sub", "own", None, None, None, None), P("sub", "own", None))
    return jax.shard_map(
        per_device, mesh=mesh, in_specs=in_specs, out_specs=out_specs, check_vma=False
    )
```

time: 52.5 us -> 41.4 us (0.79)
  Pallas kernels: 17.1 us -> 9.92 us
  local copies, waits for them, and re-layouts: 4.9 us -> 0.77 us
    pallas_call x2, Pallas kernels: 15.7 us -> 8.54 us  [the longest x1 6.49 us: per_device(): pl.pallas_call(apply_kernel, name='apply', out_shape=(sent, sent, square)...]
    unnamed x11, local copies, waits for them, and re-layouts: 4.9 us -> 0.77 us
  transfers between devices with their start and end apart: 2 -> 2, of which waited for: 0 -> 0; matrix products, arithmetic and copies ran while one was open for 0% -> 0% of each run, Pallas kernels for 15% -> 5%
where the time goes in v2:
time: 41.4 us; the launch traced here: 41.1 us
  starting transfers between devices  16.9 us (41%)
  blocking collectives  12.8 us (31%)
  Pallas kernels  9.92 us (24%)
  local copies, waits for them, and re-layouts  0.77 us (2%)
  between operations  0.76 us (2%)
    ppermute x1, starting transfers between devices, per_device(): got_cross = lax.ppermute(cross, 'sub', pairs + [(j, i) for i, j in pairs])  14.9 us
    all_to_all x1, blocking collectives, per_device(): received = lax.all_to_all(tiles, 'own', 0, 0, tiled=True)  12.8 us
    pallas_call x1, Pallas kernels, per_device(): pl.pallas_call(apply_kernel, name='apply', out_shape=(sent, sent, square)...  6.49 us
    pallas_call x1, Pallas kernels, per_device(): pl.pallas_call(basis_kernel, name='basis', out_shape=basis, in_specs=[SME...  2.05 us
    ppermute x1, starting transfers between devices, per_device(): got_inner = lax.ppermute(inner, 'sub', [(i, i ^ 1) for i in range(chain)])  1.92 us
    pallas_call x1, Pallas kernels, per_device(): pl.pallas_call(pack_kernel, name='pack', out_shape=(jax.ShapeDtypeStruct(...  1.37 us
  transfers between devices with their start and end apart: 2, of which 0 were waited for; matrix products, arithmetic and copies ran while one was open for 0% of the time, Pallas kernels for 5%

profile of v2, /device:TPU:56, one launch (start us, length us, event | category | flops | bytes accessed | tf_op | source)
XLA Modules:
  0.0 41.1 jit_solution(6056614528586183783)
XLA Ops:
  0.6 0.0 copy-start.2
  0.6 0.0 copy-start
  0.7 0.0 copy-start.3
  0.7 0.0 copy-start.4
  0.7 6.5 %apply.1 = (bf16[528,128]{1,0:T(8,128)(2,1)}, bf16[528,128]{1,0:T(8,128)(2,1)}, f32[128,128]{1,0:T(8,128)}) custom-call(s32[2,512]{1,0:T(2,128)} %bitcast.11, bf16[8192,128]{1,0:T(8,128)(2,1)} %bitcast.9, bf16[64,64,128]{2,1,0:T(8,128)(2,1)} %bitcast.17, f32[1,128]{1,0:T(1,128)} %bitcast.13), custom_call_target="tpu_custom_call" | custom-call | flops 536870912 | bytes 4194304 | tf_op jit(solution)/shard_map/apply/pallas_call | solution.py:165
  7.2 0.0 copy-start.1
  7.2 14.9 %collective-permute-start = (bf16[528,128]{1,0:T(8,128)(2,1)}, bf16[528,128]{1,0:T(8,128)(2,1)S(1)}, u32[]{:S(2)}, u32[]{:S(2)}) collective-permute-start(bf16[528,128]{1,0:T(8,128)(2,1)} %get-tuple-element.7), channel_id=1, source_target_pairs={{4,8},{12,16},{20,24},{28,32},{36,40},{44,48},{52,56},{60,64},{68,... | collective-permute-start | bytes 405512 | tf_op jit(solution)/shard_map/ppermute | solution.py:186
  22.1 1.9 %collective-permute-start.1 = (bf16[528,128]{1,0:T(8,128)(2,1)}, bf16[528,128]{1,0:T(8,128)(2,1)S(1)}, u32[]{:S(2)}, u32[]{:S(2)}) collective-permute-start(bf16[528,128]{1,0:T(8,128)(2,1)} %get-tuple-element.8), channel_id=1, source_target_pairs={{0,4},{4,0},{8,12},{12,8},{16,20},{20,16},{24,28},{28,24},{32,36},... | collective-permute-start | bytes 405512 | tf_op jit(solution)/shard_map/ppermute | solution.py:187
  24.0 0.0 copy-done.2
  24.1 0.0 copy-done
  24.1 2.0 %basis.1.zt = bf16[128,1024]{1,0:T(8,128)(2,1)S(1)} custom-call(s32[2,512]{1,0:T(2,128)S(1)} %bitcast.12, bf16[8192,128]{1,0:T(8,128)(2,1)S(1)} %bitcast.10), custom_call_target="tpu_custom_call" | custom-call | flops 268435456 | bytes 2097152 | tf_op jit(solution)/shard_map/basis/pallas_call | solution.py:188
  26.1 0.0 collective-permute-done.cross
  26.1 0.0 collective-permute-done.1.inner
  26.1 0.0 copy-done.3
  26.2 0.0 copy-done.4
  26.2 0.0 copy-done.1
  26.2 1.4 %pack.1 = (f32[4,8,8,384]{3,2,1,0:T(8,128)S(1)}, f32[1,128]{1,0:T(1,128)}) custom-call(s32[1,16]{1,0:T(1,128)S(1)} %bitcast.15, bf16[528,128]{1,0:T(8,128)(2,1)S(1)} %collective-permute-done.cross, bf16[528,128]{1,0:T(8,128)(2,1)S(1)} %collective-permute-done.1.inner, bf16[128,1024]{1,0:T(8,128)(2,1)S(1)} %basis.1.zt, f32[128,128]{1,0:T(8,128)S(1)} %copy-done.1, ...), custom_call_target="tpu_custom_call" | custom-call | tf_op jit(solution)/shard_map/pack/pallas_call | solution.py:198
  27.6 12.8 %all_to_all.5 = f32[4,8,8,384]{3,2,1,0:T(8,128)S(1)} all-to-all(f32[4,8,8,384]{3,2,1,0:T(8,128)S(1)} %get-tuple-element.10), channel_id=1, replica_groups=mesh['sub'=192,'own'=4] {'own'}, dimensions={0} | all-to-all | bytes 786432 | tf_op jit(solution)/shard_map/all_to_all | solution.py:210
  40.4 0.7 %copy.8 = f32[1,1,4,8,8,384]{5,4,3,2,1,0:T(8,128)} copy(f32[1,1,4,8,8,384]{5,4,3,2,1,0:T(8,128)S(1)} %bitcast.16) | data formatting | bytes 786432
Async XLA Ops:
  0.6 23.4 %copy-start.2 = (s32[1,1,2,512]{3,2,1,0:T(2,128)S(1)}, s32[1,1,2,512]{3,2,1,0:T(2,128)}, u32[]{:S(2)}) copy-start(s32[1,1,2,512]{3,2,1,0:T(2,128)} %param.7) | copy-start | bytes 12292
  0.6 23.4 %copy-start = (bf16[1,1,8192,128]{3,2,1,0:T(8,128)(2,1)S(1)}, bf16[1,1,8192,128]{3,2,1,0:T(8,128)(2,1)}, u32[]{:S(2)}) copy-start(bf16[1,1,8192,128]{3,2,1,0:T(8,128)(2,1)} %param.5) | copy-start | bytes 6291460
  0.7 25.5 %copy-start.3 = (f32[1,1,128]{2,1,0:T(1,128)S(1)}, f32[1,1,128]{2,1,0:T(1,128)}, u32[]{:S(2)}) copy-start(f32[1,1,128]{2,1,0:T(1,128)} %param.9) | copy-start | bytes 1540
  0.7 25.5 %copy-start.4 = (s32[1,1,16,1]{2,3,1,0:T(1,128)S(1)}, s32[1,1,16,1]{2,3,1,0:T(1,128)}, u32[]{:S(2)}) copy-start(s32[1,1,16,1]{2,3,1,0:T(1,128)} %param.8) | copy-start | bytes 196
  7.2 19.0 %copy-start.1 = (f32[128,128]{1,0:T(8,128)S(1)}, f32[128,128]{1,0:T(8,128)}, u32[]{:S(2)}) copy-start(f32[128,128]{1,0:T(8,128)} %get-tuple-element.9.self_block) | copy-start | bytes 196612
  7.2 18.9 %collective-permute-start = (bf16[528,128]{1,0:T(8,128)(2,1)}, bf16[528,128]{1,0:T(8,128)(2,1)S(1)}, u32[]{:S(2)}, u32[]{:S(2)}) collective-permute-start(bf16[528,128]{1,0:T(8,128)(2,1)} %get-tuple-element.7), channel_id=1, source_target_pairs={{4,8},{12,16},{20,24},{28,32},{36,40},{44,48},{52,56},{60,64},{68,... | collective-permute-start | bytes 405512 | tf_op jit(solution)/shard_map/ppermute | solution.py:186
  22.1 4.0 %collective-permute-start.1 = (bf16[528,128]{1,0:T(8,128)(2,1)}, bf16[528,128]{1,0:T(8,128)(2,1)S(1)}, u32[]{:S(2)}, u32[]{:S(2)}) collective-permute-start(bf16[528,128]{1,0:T(8,128)(2,1)} %get-tuple-element.8), channel_id=1, source_target_pairs={{0,4},{4,0},{8,12},{12,8},{16,20},{20,16},{24,28},{28,24},{32,36},... | collective-permute-start | bytes 405512 | tf_op jit(solution)/shard_map/ppermute | solution.py:187

commit v3 on v2

--- a/solution.py
+++ b/solution.py
@@ -8,9 +8,9 @@
 TR = 8
 SCAP = 8
 PAD = 16
-STEP = 512
+STEP = 1024
 A_CUTS = 2
-Z_CUTS = 4
+Z_CUTS = 2
 ROOM = 58 << 20
 BASIS_ROOM = 40 << 20
 PACK_ROOM = 16 << 20
@@ -39,7 +39,7 @@
 
 
 def apply_kernel(
-    idx_hbm, z_hbm, a_hbm, vec, cross, inner, self_block, idx, z_v, a_v, x_v, w_v, rows_v, sent, self_v, sems
+    idx_hbm, z_hbm, a_hbm, vec, cross, inner, self_block, z_v, idx, a_v, x_v, w_v, rows_v, sems
 ):
     order, _, nb = a_v.shape
     half = order // 2
@@ -66,7 +66,7 @@
         copies_z[-1].start()
     extra = split3(vec[...])
     for side in range(2):
-        sent[side, pl.ds(count, PAD), :] = extra
+        (cross, inner)[side][pl.ds(count, PAD), :] = extra
     for c in range(A_CUTS):
         copies_a[2 * c].wait()
         copies_a[2 * c + 1].wait()
@@ -86,14 +86,12 @@
         )
         out = jnp.dot(left, right, preferred_element_type=F32)
         w_v[pl.ds(at, order), :] = jnp.concatenate([out[:, :lanes], out[:, lanes:]], axis=0)
-    mine = parity()
-    leaving = []
-    for slot, target in enumerate((cross, inner)):
-        rows = rows_v.at[pl.ds(slot * count, count)]
-        gather_rows(idx, mine if slot == 0 else 1 - mine, w_v, rows)
-        sent[slot, pl.ds(0, count), :] = rows[...].astype(BF16)
-        leaving.append(pltpu.make_async_copy(sent.at[slot], target, sems.at[slot]))
-        leaving[-1].start()
+    for side in range(2):
+        gather_rows(idx, side, w_v, rows_v.at[pl.ds(side * count, count)])
+    low, high = rows_v[pl.ds(0, count), :].astype(BF16), rows_v[pl.ds(count, count), :].astype(BF16)
+    even = parity() == 0
+    cross[pl.ds(0, count), :] = jnp.where(even, low, high)
+    inner[pl.ds(0, count), :] = jnp.where(even, high, low)
     total = jnp.zeros((lanes, lanes), F32)
     for at in range(0, n, STEP):
         total += lax.dot_general(
@@ -102,21 +100,16 @@
             (((0,), (0,)), ((), ())),
             preferred_element_type=F32,
         )
-    self_v[...] = total
-    leaving.append(pltpu.make_async_copy(self_v, self_block, sems.at[2]))
-    leaving[-1].start()
-    for copy in leaving:
-        copy.wait()
+    self_block[...] = total
 
 
 def basis_kernel(idx, z, zt, z_f, rows_v):
     count = idx.shape[1]
-    mine = parity()
     for at in range(0, z.shape[0], STEP):
         z_f[pl.ds(at, STEP), :] = z[pl.ds(at, STEP), :].astype(F32)
     for slot in range(2):
         rows = rows_v.at[pl.ds(slot * count, count)]
-        gather_rows(idx, mine if slot == 0 else 1 - mine, z_f, rows)
+        gather_rows(idx, slot, z_f, rows)
     zt[...] = rows_v[...].astype(BF16).T
 
 
@@ -130,8 +123,10 @@
         return extra[0:1] + (extra[1:2] + extra[2:3])
 
     tiles[...] = jnp.zeros_like(tiles)
-    by_cross = jnp.dot(zt[:, :count], cross[pl.ds(0, count), :], preferred_element_type=F32)
-    by_inner = jnp.dot(zt[:, count:], inner[pl.ds(0, count), :], preferred_element_type=F32)
+    near = pl.multiple_of(mine * count, count)
+    far = pl.multiple_of((1 - mine) * count, count)
+    by_cross = jnp.dot(zt[:, pl.ds(near, count)], cross[pl.ds(0, count), :], preferred_element_type=F32)
+    by_inner = jnp.dot(zt[:, pl.ds(far, count)], inner[pl.ds(0, count), :], preferred_element_type=F32)
     own = self_block[...]
     at = pl.multiple_of(mine * (2 * lanes), lanes)
     row_v[:, pl.ds(at, lanes)] = by_cross
@@ -159,24 +154,20 @@
     count = idx.shape[1]
     chain = lax.axis_size("sub")
     owners = lax.axis_size("own")
-    sent = jax.ShapeDtypeStruct((count + PAD, lanes), BF16)
-    square = jax.ShapeDtypeStruct((lanes, lanes), F32)
+    sent = pltpu.VMEM((count + PAD, lanes), BF16)
     basis = jax.ShapeDtypeStruct((lanes, 2 * count), BF16)
-    cross, inner, self_block = pl.pallas_call(
+    cross, inner, self_block, z = pl.pallas_call(
         apply_kernel,
         name="apply",
-        out_shape=(sent, sent, square),
+        out_shape=(sent, sent, pltpu.VMEM((lanes, lanes), F32), pltpu.VMEM((n, lanes), BF16)),
         in_specs=[HBM, HBM, HBM, VMEM],
-        out_specs=(HBM, HBM, HBM),
+        out_specs=(VMEM,) * 4,
         scratch_shapes=[
             pltpu.SMEM((2, count), jnp.int32),
-            pltpu.VMEM((n, lanes), BF16),
             pltpu.VMEM((order, order, nb), BF16),
             pltpu.VMEM((order // 2 * (nb + 8), 2 * order), F32),
             pltpu.VMEM((n, lanes), F32),
             pltpu.VMEM((2 * count, lanes), F32),
-            pltpu.VMEM((2, count + PAD, lanes), BF16),
-            pltpu.VMEM((lanes, lanes), F32),
             pltpu.SemaphoreType.DMA((1 + 2 * A_CUTS + Z_CUTS,)),
         ],
         compiler_params=pltpu.CompilerParams(vmem_limit_bytes=ROOM),

time: 41.4 us -> 39.3 us (0.949)
  Pallas kernels: 9.92 us -> 8.07 us
    pallas_call x1, Pallas kernels: 6.49 us -> 5.05 us  [per_device(): pl.pallas_call(apply_kernel, name='apply', out_shape=(sent, sent, pltpu.V...]
  transfers between devices with their start and end apart: 2 -> 2, of which waited for: 0 -> 0; matrix products, arithmetic and copies ran while one was open for 0% -> 0% of each run, Pallas kernels for 5% -> 4%
where the time goes in v3:
time: 39.3 us; the launch traced here: 39.1 us
  starting transfers between devices  16.7 us (42%)
  blocking collectives  12.8 us (33%)
  Pallas kernels  8.07 us (21%)
  local copies, waits for them, and re-layouts  0.76 us (2%)
  between operations  0.73 us (2%)
    ppermute x1, starting transfers between devices, per_device(): got_cross = lax.ppermute(cross, 'sub', pairs + [(j, i) for i, j in pairs])  14.8 us
    all_to_all x1, blocking collectives, per_device(): received = lax.all_to_all(tiles, 'own', 0, 0, tiled=True)  12.8 us
    pallas_call x1, Pallas kernels, per_device(): pl.pallas_call(apply_kernel, name='apply', out_shape=(sent, sent, pltpu.V...  5.05 us
    ppermute x1, starting transfers between devices, per_device(): got_inner = lax.ppermute(inner, 'sub', [(i, i ^ 1) for i in range(chain)])  1.92 us
    pallas_call x1, Pallas kernels, per_device(): pl.pallas_call(basis_kernel, name='basis', out_shape=basis, in_specs=[SME...  1.64 us
    pallas_call x1, Pallas kernels, per_device(): pl.pallas_call(pack_kernel, name='pack', out_shape=(jax.ShapeDtypeStruct(...  1.38 us
  transfers between devices with their start and end apart: 2, of which 0 were waited for; matrix products, arithmetic and copies ran while one was open for 0% of the time, Pallas kernels for 4%

profile of v3, /device:TPU:56, one launch (start us, length us, event | category | flops | bytes accessed | tf_op | source)
XLA Modules:
  0.0 39.1 jit_solution(6567537982832947906)
XLA Ops:
  0.6 0.0 copy-start
  0.6 0.0 copy-start.1
  0.7 0.0 copy-start.2
  0.7 5.0 %apply.1 = (bf16[528,128]{1,0:T(8,128)(2,1)S(1)}, bf16[528,128]{1,0:T(8,128)(2,1)S(1)}, f32[128,128]{1,0:T(8,128)S(1)}, bf16[8192,128]{1,0:T(8,128)(2,1)S(1)}) custom-call(s32[2,512]{1,0:T(2,128)} %bitcast.9, bf16[8192,128]{1,0:T(8,128)(2,1)} %bitcast.14, bf16[64,64,128]{2,1,0:T(8,128)(2,1)} %bitcast.16, f32[1,128]{1,0:T(1,128)} %bitcast.11), custom_call_target="tpu_custom_call" | custom-call | flops 536870912 | bytes 4194304 | tf_op jit(solution)/shard_map/apply/pallas_call | solution.py:159
  5.7 14.8 %collective-permute-start = (bf16[528,128]{1,0:T(8,128)(2,1)S(1)}, bf16[528,128]{1,0:T(8,128)(2,1)S(1)}, u32[]{:S(2)}, u32[]{:S(2)}) collective-permute-start(bf16[528,128]{1,0:T(8,128)(2,1)S(1)} %get-tuple-element.8), channel_id=1, source_target_pairs={{4,8},{12,16},{20,24},{28,32},{36,40},{44,48},{52,56},{60,64},{68,... | collective-permute-start | bytes 405512 | tf_op jit(solution)/shard_map/ppermute | solution.py:177
  20.5 1.9 %collective-permute-start.1 = (bf16[528,128]{1,0:T(8,128)(2,1)S(1)}, bf16[528,128]{1,0:T(8,128)(2,1)S(1)}, u32[]{:S(2)}, u32[]{:S(2)}) collective-permute-start(bf16[528,128]{1,0:T(8,128)(2,1)S(1)} %get-tuple-element.9), channel_id=1, source_target_pairs={{0,4},{4,0},{8,12},{12,8},{16,20},{20,16},{24,28},{28,24},{32,36},... | collective-permute-start | bytes 405512 | tf_op jit(solution)/shard_map/ppermute | solution.py:178
  22.5 0.0 copy-done
  22.5 1.6 %basis.1.zt = bf16[128,1024]{1,0:T(8,128)(2,1)S(1)} custom-call(s32[2,512]{1,0:T(2,128)S(1)} %bitcast.10, bf16[8192,128]{1,0:T(8,128)(2,1)S(1)} %get-tuple-element.10.z), custom_call_target="tpu_custom_call" | custom-call | flops 268435456 | bytes 2097152 | tf_op jit(solution)/shard_map/basis/pallas_call | solution.py:179
  24.1 0.0 collective-permute-done.cross
  24.1 0.0 collective-permute-done.1.inner
  24.1 0.0 copy-done.1
  24.2 0.0 copy-done.2
  24.2 1.4 %pack.1 = (f32[4,8,8,384]{3,2,1,0:T(8,128)S(1)}, f32[1,128]{1,0:T(1,128)}) custom-call(s32[1,16]{1,0:T(1,128)S(1)} %bitcast.13, bf16[528,128]{1,0:T(8,128)(2,1)S(1)} %collective-permute-done.cross, bf16[528,128]{1,0:T(8,128)(2,1)S(1)} %collective-permute-done.1.inner, bf16[128,1024]{1,0:T(8,128)(2,1)S(1)} %basis.1.zt, ...), custom_call_target="tpu_custom_call" | custom-call | tf_op jit(solution)/shard_map/pack/pallas_call | solution.py:189
  25.5 12.8 %all_to_all.5 = f32[4,8,8,384]{3,2,1,0:T(8,128)S(1)} all-to-all(f32[4,8,8,384]{3,2,1,0:T(8,128)S(1)} %get-tuple-element.12), channel_id=1, replica_groups=mesh['sub'=192,'own'=4] {'own'}, dimensions={0} | all-to-all | bytes 786432 | tf_op jit(solution)/shard_map/all_to_all | solution.py:201
  38.4 0.7 %copy.8 = f32[1,1,4,8,8,384]{5,4,3,2,1,0:T(8,128)} copy(f32[1,1,4,8,8,384]{5,4,3,2,1,0:T(8,128)S(1)} %bitcast.15) | data formatting | bytes 786432
Async XLA Ops:
  0.6 21.8 %copy-start = (s32[1,1,2,512]{3,2,1,0:T(2,128)S(1)}, s32[1,1,2,512]{3,2,1,0:T(2,128)}, u32[]{:S(2)}) copy-start(s32[1,1,2,512]{3,2,1,0:T(2,128)} %param.7) | copy-start | bytes 12292
  0.6 23.5 %copy-start.1 = (f32[1,1,128]{2,1,0:T(1,128)S(1)}, f32[1,1,128]{2,1,0:T(1,128)}, u32[]{:S(2)}) copy-start(f32[1,1,128]{2,1,0:T(1,128)} %param.9) | copy-start | bytes 1540
  0.7 23.5 %copy-start.2 = (s32[1,1,16,1]{2,3,1,0:T(1,128)S(1)}, s32[1,1,16,1]{2,3,1,0:T(1,128)}, u32[]{:S(2)}) copy-start(s32[1,1,16,1]{2,3,1,0:T(1,128)} %param.8) | copy-start | bytes 196
  5.7 18.4 %collective-permute-start = (bf16[528,128]{1,0:T(8,128)(2,1)S(1)}, bf16[528,128]{1,0:T(8,128)(2,1)S(1)}, u32[]{:S(2)}, u32[]{:S(2)}) collective-permute-start(bf16[528,128]{1,0:T(8,128)(2,1)S(1)} %get-tuple-element.8), channel_id=1, source_target_pairs={{4,8},{12,16},{20,24},{28,32},{36,40},{44,48},{52,56},{60,64},{68,... | collective-permute-start | bytes 405512 | tf_op jit(solution)/shard_map/ppermute | solution.py:177
  20.5 3.6 %collective-permute-start.1 = (bf16[528,128]{1,0:T(8,128)(2,1)S(1)}, bf16[528,128]{1,0:T(8,128)(2,1)S(1)}, u32[]{:S(2)}, u32[]{:S(2)}) collective-permute-start(bf16[528,128]{1,0:T(8,128)(2,1)S(1)} %get-tuple-element.9), channel_id=1, source_target_pairs={{0,4},{4,0},{8,12},{12,8},{16,20},{20,16},{24,28},{28,24},{32,36},... | collective-permute-start | bytes 405512 | tf_op jit(solution)/shard_map/ppermute | solution.py:178

commit v4 on v3

--- a/solution.py
+++ b/solution.py
@@ -9,6 +9,7 @@
 SCAP = 8
 PAD = 16
 STEP = 1024
+LAP = 24
 A_CUTS = 2
 Z_CUTS = 2
 ROOM = 58 << 20
@@ -25,6 +26,10 @@
     return lax.rem(lax.axis_index("sub"), 2)
 
 
+def early():
+    return lax.rem(lax.axis_index("sub"), LAP) < 2
+
+
 def split3(x):
     hi = x.astype(BF16)
     rest = x - hi.astype(F32)
@@ -39,7 +44,7 @@
 
 
 def apply_kernel(
-    idx_hbm, z_hbm, a_hbm, vec, cross, inner, self_block, z_v, idx, a_v, x_v, w_v, rows_v, sems
+    idx_hbm, z_hbm, a_hbm, vec, cross, inner, self_block, z_v, zt, idx, a_v, x_v, w_v, rows_v, sems
 ):
     order, _, nb = a_v.shape
     half = order // 2
@@ -102,15 +107,30 @@
         )
     self_block[...] = total
 
-
-def basis_kernel(idx, z, zt, z_f, rows_v):
+    @pl.when(early())
+    def _():
+        basis_rows(idx, z_v, w_v, rows_v, zt)
+
+
+def basis_rows(idx, z, z_f, rows_v, zt):
     count = idx.shape[1]
     for at in range(0, z.shape[0], STEP):
         z_f[pl.ds(at, STEP), :] = z[pl.ds(at, STEP), :].astype(F32)
-    for slot in range(2):
-        rows = rows_v.at[pl.ds(slot * count, count)]
-        gather_rows(idx, slot, z_f, rows)
+    for side in range(2):
+        gather_rows(idx, side, z_f, rows_v.at[pl.ds(side * count, count)])
     zt[...] = rows_v[...].astype(BF16).T
+
+
+def basis_kernel(idx, z, given, zt, z_f, rows_v):
+    ahead = early()
+
+    @pl.when(ahead)
+    def _():
+        zt[...] = given[...]
+
+    @pl.when(jnp.logical_not(ahead))
+    def _():
+        basis_rows(idx, z, z_f, rows_v, zt)
 
 
 def pack_kernel(owner, cross, inner, zt, self_block, vec, tiles, product, row_v, used):
@@ -155,13 +175,13 @@
     chain = lax.axis_size("sub")
     owners = lax.axis_size("own")
     sent = pltpu.VMEM((count + PAD, lanes), BF16)
-    basis = jax.ShapeDtypeStruct((lanes, 2 * count), BF16)
-    cross, inner, self_block, z = pl.pallas_call(
+    basis = pltpu.VMEM((lanes, 2 * count), BF16)
+    cross, inner, self_block, z, given = pl.pallas_call(
         apply_kernel,
         name="apply",
-        out_shape=(sent, sent, pltpu.VMEM((lanes, lanes), F32), pltpu.VMEM((n, lanes), BF16)),
+        out_shape=(sent, sent, pltpu.VMEM((lanes, lanes), F32), pltpu.VMEM((n, lanes), BF16), basis),
         in_specs=[HBM, HBM, HBM, VMEM],
-        out_specs=(VMEM,) * 4,
+        out_specs=(VMEM,) * 5,
         scratch_shapes=[
             pltpu.SMEM((2, count), jnp.int32),
             pltpu.VMEM((order, order, nb), BF16),
@@ -180,12 +200,12 @@
         basis_kernel,
         name="basis",
         out_shape=basis,
-        in_specs=[SMEM, VMEM],
+        in_specs=[SMEM, VMEM, VMEM],
         out_specs=VMEM,
         scratch_shapes=[pltpu.VMEM((n, lanes), F32), pltpu.VMEM((2 * count, lanes), F32)],
         compiler_params=pltpu.CompilerParams(vmem_limit_bytes=BASIS_ROOM),
         cost_estimate=pl.CostEstimate(flops=1 << 28, bytes_accessed=2 << 20, transcendentals=0),
-    )(idx, z)
+    )(idx, z, given)
     tiles, product = pl.pallas_call(
         pack_kernel,
         name="pack",

time: 39.3 us -> 38.6 us (0.982)
  starting transfers between devices: 16.7 us -> 15.7 us
  waiting for transfers between devices: 0.01 us -> 0.66 us
    ppermute x1, starting transfers between devices: 14.8 us -> 13.8 us  [per_device(): got_cross = lax.ppermute(cross, 'sub', pairs + [(j, i) for i, j in pairs])]
    pallas_call x1, Pallas kernels: 1.64 us -> 0.65 us  [per_device(): pl.pallas_call(basis_kernel, name='basis', out_shape=basis, in_specs=[SME...]
    pallas_call x1, Pallas kernels: 5.05 us -> 6.04 us  [per_device(): pl.pallas_call(apply_kernel, name='apply', out_shape=(sent, sent, pltpu.V...]
    ppermute x1, waiting for transfers between devices: 0.01 us -> 0.57 us  [per_device(): got_inner = lax.ppermute(inner, 'sub', [(i, i ^ 1) for i in range(chain)])]
  transfers between devices with their start and end apart: 2 -> 2, of which waited for: 0 -> 2; matrix products, arithmetic and copies ran while one was open for 0% -> 0% of each run, Pallas kernels for 4% -> 2%
where the time goes in v4:
time: 38.6 us; the launch traced here: 38.3 us
  starting transfers between devices  15.7 us (41%)
  blocking collectives  12.5 us (32%)
  Pallas kernels  8.06 us (21%)
  local copies, waits for them, and re-layouts  0.76 us (2%)
  between operations  0.7 us (2%)
  waiting for transfers between devices  0.66 us (2%)
    ppermute x1, starting transfers between devices, per_device(): got_cross = lax.ppermute(cross, 'sub', pairs + [(j, i) for i, j in pairs])  13.8 us
    all_to_all x1, blocking collectives, per_device(): received = lax.all_to_all(tiles, 'own', 0, 0, tiled=True)  12.5 us
    pallas_call x1, Pallas kernels, per_device(): pl.pallas_call(apply_kernel, name='apply', out_shape=(sent, sent, pltpu.V...  6.04 us
    ppermute x1, starting transfers between devices, per_device(): got_inner = lax.ppermute(inner, 'sub', [(i, i ^ 1) for i in range(chain)])  1.92 us
    pallas_call x1, Pallas kernels, per_device(): pl.pallas_call(pack_kernel, name='pack', out_shape=(jax.ShapeDtypeStruct(...  1.38 us
  transfers between devices with their start and end apart: 2, of which 2 were waited for; matrix products, arithmetic and copies ran while one was open for 0% of the time, Pallas kernels for 2%

profile of v4, /device:TPU:56, one launch (start us, length us, event | category | flops | bytes accessed | tf_op | source)
XLA Modules:
  0.0 38.3 jit_solution(5914107004959588415)
XLA Ops:
  0.6 0.0 copy-start
  0.6 6.0 %apply.1 = (bf16[528,128]{1,0:T(8,128)(2,1)S(1)}, bf16[528,128]{1,0:T(8,128)(2,1)S(1)}, f32[128,128]{1,0:T(8,128)S(1)}, bf16[8192,128]{1,0:T(8,128)(2,1)S(1)}, bf16[128,1024]{1,0:T(8,128)(2,1)S(1)}) custom-call(s32[2,512]{1,0:T(2,128)} %bitcast.9, bf16[8192,128]{1,0:T(8,128)(2,1)} %bitcast.14, bf16[64,64,128]{2,1,0:T(8,128)(2,1)} %bitcast.16, f32[1,128]{1,0:T(1,128)} %bitcast.11), custom_call_target="tpu_custom_call" | custom-call | flops 536870912 | bytes 4194304 | tf_op jit(solution)/shard_map/apply/pallas_call | solution.py:179
  6.7 0.0 copy-start.1
  6.7 0.0 copy-start.2
  6.7 13.8 %collective-permute-start = (bf16[528,128]{1,0:T(8,128)(2,1)S(1)}, bf16[528,128]{1,0:T(8,128)(2,1)S(1)}, u32[]{:S(2)}, u32[]{:S(2)}) collective-permute-start(bf16[528,128]{1,0:T(8,128)(2,1)S(1)} %get-tuple-element.9), channel_id=1, source_target_pairs={{4,8},{12,16},{20,24},{28,32},{36,40},{44,48},{52,56},{60,64},{68,... | collective-permute-start | bytes 405512 | tf_op jit(solution)/shard_map/ppermute | solution.py:197
  20.5 1.9 %collective-permute-start.1 = (bf16[528,128]{1,0:T(8,128)(2,1)S(1)}, bf16[528,128]{1,0:T(8,128)(2,1)S(1)}, u32[]{:S(2)}, u32[]{:S(2)}) collective-permute-start(bf16[528,128]{1,0:T(8,128)(2,1)S(1)} %get-tuple-element.10), channel_id=1, source_target_pairs={{0,4},{4,0},{8,12},{12,8},{16,20},{20,16},{24,28},{28,24},{32,36},... | collective-permute-start | bytes 405512 | tf_op jit(solution)/shard_map/ppermute | solution.py:198
  22.4 0.0 copy-done
  22.4 0.6 %basis.1.zt = bf16[128,1024]{1,0:T(8,128)(2,1)S(1)} custom-call(s32[2,512]{1,0:T(2,128)S(1)} %bitcast.10, bf16[8192,128]{1,0:T(8,128)(2,1)S(1)} %get-tuple-element.11.z, bf16[128,1024]{1,0:T(8,128)(2,1)S(1)} %get-tuple-element.12.given), custom_call_target="tpu_custom_call" | custom-call | flops 268435456 | bytes 2097152 | tf_op jit(solution)/shard_map/basis/pallas_call | solution.py:199
  23.1 0.1 collective-permute-done.cross
  23.2 0.6 %collective-permute-done.1.inner = bf16[528,128]{1,0:T(8,128)(2,1)S(1)} collective-permute-done((bf16[528,128]{1,0:T(8,128)(2,1)S(1)}, bf16[528,128]{1,0:T(8,128)(2,1)S(1)}, u32[]{:S(2)}, u32[]{:S(2)}) %collective-permute-start.1) | collective-permute-done | bytes 135200 | tf_op jit(solution)/shard_map/ppermute | solution.py:198
  23.7 0.0 copy-done.1
  23.7 0.0 copy-done.2
  23.7 1.4 %pack.1 = (f32[4,8,8,384]{3,2,1,0:T(8,128)S(1)}, f32[1,128]{1,0:T(1,128)}) custom-call(s32[1,16]{1,0:T(1,128)S(1)} %bitcast.13, bf16[528,128]{1,0:T(8,128)(2,1)S(1)} %collective-permute-done.cross, bf16[528,128]{1,0:T(8,128)(2,1)S(1)} %collective-permute-done.1.inner, bf16[128,1024]{1,0:T(8,128)(2,1)S(1)} %basis.1.zt, ...), custom_call_target="tpu_custom_call" | custom-call | tf_op jit(solution)/shard_map/pack/pallas_call | solution.py:209
  25.1 12.5 %all_to_all.5 = f32[4,8,8,384]{3,2,1,0:T(8,128)S(1)} all-to-all(f32[4,8,8,384]{3,2,1,0:T(8,128)S(1)} %get-tuple-element.14), channel_id=1, replica_groups=mesh['sub'=192,'own'=4] {'own'}, dimensions={0} | all-to-all | bytes 786432 | tf_op jit(solution)/shard_map/all_to_all | solution.py:221
  37.6 0.7 %copy.8 = f32[1,1,4,8,8,384]{5,4,3,2,1,0:T(8,128)} copy(f32[1,1,4,8,8,384]{5,4,3,2,1,0:T(8,128)S(1)} %bitcast.15) | data formatting | bytes 786432
Async XLA Ops:
  0.6 21.8 %copy-start = (s32[1,1,2,512]{3,2,1,0:T(2,128)S(1)}, s32[1,1,2,512]{3,2,1,0:T(2,128)}, u32[]{:S(2)}) copy-start(s32[1,1,2,512]{3,2,1,0:T(2,128)} %param.7) | copy-start | bytes 12292
  6.7 17.1 %copy-start.1 = (f32[1,1,128]{2,1,0:T(1,128)S(1)}, f32[1,1,128]{2,1,0:T(1,128)}, u32[]{:S(2)}) copy-start(f32[1,1,128]{2,1,0:T(1,128)} %param.9) | copy-start | bytes 1540
  6.7 17.0 %copy-start.2 = (s32[1,1,16,1]{2,3,1,0:T(1,128)S(1)}, s32[1,1,16,1]{2,3,1,0:T(1,128)}, u32[]{:S(2)}) copy-start(s32[1,1,16,1]{2,3,1,0:T(1,128)} %param.8) | copy-start | bytes 196
  6.7 16.5 %collective-permute-start = (bf16[528,128]{1,0:T(8,128)(2,1)S(1)}, bf16[528,128]{1,0:T(8,128)(2,1)S(1)}, u32[]{:S(2)}, u32[]{:S(2)}) collective-permute-start(bf16[528,128]{1,0:T(8,128)(2,1)S(1)} %get-tuple-element.9), channel_id=1, source_target_pairs={{4,8},{12,16},{20,24},{28,32},{36,40},{44,48},{52,56},{60,64},{68,... | collective-permute-start | bytes 405512 | tf_op jit(solution)/shard_map/ppermute | solution.py:197
  20.5 3.2 %collective-permute-start.1 = (bf16[528,128]{1,0:T(8,128)(2,1)S(1)}, bf16[528,128]{1,0:T(8,128)(2,1)S(1)}, u32[]{:S(2)}, u32[]{:S(2)}) collective-permute-start(bf16[528,128]{1,0:T(8,128)(2,1)S(1)} %get-tuple-element.10), channel_id=1, source_target_pairs={{0,4},{4,0},{8,12},{12,8},{16,20},{20,16},{24,28},{28,24},{32,36},... | collective-permute-start | bytes 405512 | tf_op jit(solution)/shard_map/ppermute | solution.py:198

commit v5 on v4

--- a/solution.py
+++ b/solution.py
@@ -44,7 +44,7 @@
 
 
 def apply_kernel(
-    idx_hbm, z_hbm, a_hbm, vec, cross, inner, self_block, z_v, zt, idx, a_v, x_v, w_v, rows_v, sems
+    idx_hbm, z_hbm, a_hbm, vec, cross, inner, self_block, z_v, zt, applied, idx, a_v, x_v, w_v, rows_v, sems
 ):
     order, _, nb = a_v.shape
     half = order // 2
@@ -90,26 +90,32 @@
             [jnp.concatenate([zb, zero], axis=1), jnp.concatenate([zero, zb], axis=1)], axis=0
         )
         out = jnp.dot(left, right, preferred_element_type=F32)
-        w_v[pl.ds(at, order), :] = jnp.concatenate([out[:, :lanes], out[:, lanes:]], axis=0)
+        out = jnp.concatenate([out[:, :lanes], out[:, lanes:]], axis=0)
+        w_v[pl.ds(at, order), :] = out
+        applied[pl.ds(at, order), :] = out.astype(BF16)
     for side in range(2):
         gather_rows(idx, side, w_v, rows_v.at[pl.ds(side * count, count)])
     low, high = rows_v[pl.ds(0, count), :].astype(BF16), rows_v[pl.ds(count, count), :].astype(BF16)
     even = parity() == 0
     cross[pl.ds(0, count), :] = jnp.where(even, low, high)
     inner[pl.ds(0, count), :] = jnp.where(even, high, low)
-    total = jnp.zeros((lanes, lanes), F32)
-    for at in range(0, n, STEP):
+
+    @pl.when(early())
+    def _():
+        self_rows(z_v, applied, self_block)
+        basis_rows(idx, z_v, w_v, rows_v, zt)
+
+
+def self_rows(z, applied, self_block):
+    total = jnp.zeros(self_block.shape, F32)
+    for at in range(0, z.shape[0], STEP):
         total += lax.dot_general(
-            z_v[pl.ds(at, STEP), :],
-            w_v[pl.ds(at, STEP), :].astype(BF16),
+            z[pl.ds(at, STEP), :],
+            applied[pl.ds(at, STEP), :],
             (((0,), (0,)), ((), ())),
             preferred_element_type=F32,
         )
     self_block[...] = total
-
-    @pl.when(early())
-    def _():
-        basis_rows(idx, z_v, w_v, rows_v, zt)
 
 
 def basis_rows(idx, z, z_f, rows_v, zt):
@@ -121,15 +127,17 @@
     zt[...] = rows_v[...].astype(BF16).T
 
 
-def basis_kernel(idx, z, given, zt, z_f, rows_v):
+def basis_kernel(idx, z, applied, given, given_self, zt, self_block, z_f, rows_v):
     ahead = early()
 
     @pl.when(ahead)
     def _():
         zt[...] = given[...]
+        self_block[...] = given_self[...]
 
     @pl.when(jnp.logical_not(ahead))
     def _():
+        self_rows(z, applied, self_block)
         basis_rows(idx, z, z_f, rows_v, zt)
 
 
@@ -175,13 +183,14 @@
     chain = lax.axis_size("sub")
     owners = lax.axis_size("own")
     sent = pltpu.VMEM((count + PAD, lanes), BF16)
+    square = pltpu.VMEM((lanes, lanes), F32)
     basis = pltpu.VMEM((lanes, 2 * count), BF16)
-    cross, inner, self_block, z, given = pl.pallas_call(
+    cross, inner, given_self, z, given, applied = pl.pallas_call(
         apply_kernel,
         name="apply",
-        out_shape=(sent, sent, pltpu.VMEM((lanes, lanes), F32), pltpu.VMEM((n, lanes), BF16), basis),
+        out_shape=(sent, sent, square, pltpu.VMEM((n, lanes), BF16), basis, pltpu.VMEM((n, lanes), BF16)),
         in_specs=[HBM, HBM, HBM, VMEM],
-        out_specs=(VMEM,) * 5,
+        out_specs=(VMEM,) * 6,
         scratch_shapes=[
             pltpu.SMEM((2, count), jnp.int32),
             pltpu.VMEM((order, order, nb), BF16),
@@ -196,16 +205,16 @@
     pairs = [(i, i + 1) for i in range(1, chain - 1, 2)]
     got_cross = lax.ppermute(cross, "sub", pairs + [(j, i) for i, j in pairs])
     got_inner = lax.ppermute(inner, "sub", [(i, i ^ 1) for i in range(chain)])
-    zt = pl.pallas_call(
+    zt, self_block = pl.pallas_call(
         basis_kernel,
         name="basis",
-        out_shape=basis,
-        in_specs=[SMEM, VMEM, VMEM],
-        out_specs=VMEM,
+        out_shape=(basis, square),
+        in_specs=[SMEM] + [VMEM] * 4,
+        out_specs=(VMEM, VMEM),
         scratch_shapes=[pltpu.VMEM((n, lanes), F32), pltpu.VMEM((2 * count, lanes), F32)],
         compiler_params=pltpu.CompilerParams(vmem_limit_bytes=BASIS_ROOM),
         cost_estimate=pl.CostEstimate(flops=1 << 28, bytes_accessed=2 << 20, transcendentals=0),
-    )(idx, z, given)
+    )(idx, z, applied, given, given_self)
     tiles, product = pl.pallas_call(
         pack_kernel,
         name="pack",

time: 38.6 us -> 37.8 us (0.979)
  starting transfers between devices: 15.7 us -> 15.1 us
    ppermute x1, starting transfers between devices: 13.8 us -> 13.2 us  [per_device(): got_cross = lax.ppermute(cross, 'sub', pairs + [(j, i) for i, j in pairs])]
where the time goes in v5:
time: 37.8 us; the launch traced here: 37.6 us
  starting transfers between devices  15.1 us (40%)
  blocking collectives  12.5 us (33%)
  Pallas kernels  7.89 us (21%)
  local copies, waits for them, and re-layouts  0.76 us (2%)
  between operations  0.7 us (2%)
  waiting for transfers between devices  0.63 us (2%)
    ppermute x1, starting transfers between devices, per_device(): got_cross = lax.ppermute(cross, 'sub', pairs + [(j, i) for i, j in pairs])  13.2 us
    all_to_all x1, blocking collectives, per_device(): received = lax.all_to_all(tiles, 'own', 0, 0, tiled=True)  12.5 us
    pallas_call x1, Pallas kernels, per_device(): pl.pallas_call(apply_kernel, name='apply', out_shape=(sent, sent, square,...  5.87 us
    ppermute x1, starting transfers between devices, per_device(): got_inner = lax.ppermute(inner, 'sub', [(i, i ^ 1) for i in range(chain)])  1.92 us
    pallas_call x1, Pallas kernels, per_device(): pl.pallas_call(pack_kernel, name='pack', out_shape=(jax.ShapeDtypeStruct(...  1.38 us
    unnamed x7, local copies, waits for them, and re-layouts  0.76 us
  transfers between devices with their start and end apart: 2, of which 2 were waited for; matrix products, arithmetic and copies ran while one was open for 0% of the time, Pallas kernels for 2%

profile of v5, /device:TPU:56, one launch (start us, length us, event | category | flops | bytes accessed | tf_op | source)
XLA Modules:
  0.0 37.6 jit_solution(1194040209468550756)
XLA Ops:
  0.6 0.0 copy-start
  0.6 5.9 %apply.1 = (bf16[528,128]{1,0:T(8,128)(2,1)S(1)}, bf16[528,128]{1,0:T(8,128)(2,1)S(1)}, f32[128,128]{1,0:T(8,128)S(1)}, bf16[8192,128]{1,0:T(8,128)(2,1)S(1)}, b...) custom-call(s32[2,512]{1,0:T(2,128)} %bitcast.9, bf16[8192,128]{1,0:T(8,128)(2,1)} %bitcast.14, ...), custom_call_target="tpu_custom_call" | custom-call | flops 536870912 | bytes 4194304 | tf_op jit(solution)/shard_map/apply/pallas_call | solution.py:188
  6.5 13.2 %collective-permute-start = (bf16[528,128]{1,0:T(8,128)(2,1)S(1)}, bf16[528,128]{1,0:T(8,128)(2,1)S(1)}, u32[]{:S(2)}, u32[]{:S(2)}) collective-permute-start(bf16[528,128]{1,0:T(8,128)(2,1)S(1)} %get-tuple-element.12), channel_id=1, source_target_pairs={{4,8},{12,16},{20,24},{28,32},{36,40},{44,48},{52,56},{60,64},{68,... | collective-permute-start | bytes 405512 | tf_op jit(solution)/shard_map/ppermute | solution.py:206
  19.7 1.9 %collective-permute-start.1 = (bf16[528,128]{1,0:T(8,128)(2,1)S(1)}, bf16[528,128]{1,0:T(8,128)(2,1)S(1)}, u32[]{:S(2)}, u32[]{:S(2)}) collective-permute-start(bf16[528,128]{1,0:T(8,128)(2,1)S(1)} %get-tuple-element.13), channel_id=1, source_target_pairs={{0,4},{4,0},{8,12},{12,8},{16,20},{20,16},{24,28},{28,24},{32,36},... | collective-permute-start | bytes 405512 | tf_op jit(solution)/shard_map/ppermute | solution.py:207
  21.6 0.0 copy-done
  21.7 0.0 copy-start.1
  21.7 0.0 copy-start.2
  21.7 0.7 %basis.1 = (bf16[128,1024]{1,0:T(8,128)(2,1)S(1)}, f32[128,128]{1,0:T(8,128)S(1)}) custom-call(s32[2,512]{1,0:T(2,128)S(1)} %bitcast.10, bf16[8192,128]{1,0:T(8,128)(2,1)S(1)} %get-tuple-element.14.z, bf16[8192,128]{1,0:T(8,128)(2,1)S(1)} %get-tuple-element.15.applied, bf16[128,1024]{1,0:T(8,128)(2,1)S(1)} %get-tuple-element.16.given, ...), custom_call_target="tpu_custom_call" | custom-call | flops 268435456 | bytes 2097152 | tf_op jit(solution)/shard_map/basis/pallas_call | solution.py:208
  22.3 0.1 collective-permute-done.cross
  22.4 0.6 %collective-permute-done.1.inner = bf16[528,128]{1,0:T(8,128)(2,1)S(1)} collective-permute-done((bf16[528,128]{1,0:T(8,128)(2,1)S(1)}, bf16[528,128]{1,0:T(8,128)(2,1)S(1)}, u32[]{:S(2)}, u32[]{:S(2)}) %collective-permute-start.1) | collective-permute-done | bytes 135200 | tf_op jit(solution)/shard_map/ppermute | solution.py:207
  23.0 0.0 copy-done.1
  23.0 0.0 copy-done.2
  23.0 1.4 %pack.1 = (f32[4,8,8,384]{3,2,1,0:T(8,128)S(1)}, f32[1,128]{1,0:T(1,128)}) custom-call(s32[1,16]{1,0:T(1,128)S(1)} %bitcast.13, bf16[528,128]{1,0:T(8,128)(2,1)S(1)} %collective-permute-done.cross, bf16[528,128]{1,0:T(8,128)(2,1)S(1)} %collective-permute-done.1.inner, bf16[128,1024]{1,0:T(8,128)(2,1)S(1)} %get-tuple-element.18.zt, ...), custom_call_target="tpu_custom_call" | custom-call | tf_op jit(solution)/shard_map/pack/pallas_call | solution.py:218
  24.3 12.5 %all_to_all.5 = f32[4,8,8,384]{3,2,1,0:T(8,128)S(1)} all-to-all(f32[4,8,8,384]{3,2,1,0:T(8,128)S(1)} %get-tuple-element.20), channel_id=1, replica_groups=mesh['sub'=192,'own'=4] {'own'}, dimensions={0} | all-to-all | bytes 786432 | tf_op jit(solution)/shard_map/all_to_all | solution.py:230
  36.8 0.7 %copy.8 = f32[1,1,4,8,8,384]{5,4,3,2,1,0:T(8,128)} copy(f32[1,1,4,8,8,384]{5,4,3,2,1,0:T(8,128)S(1)} %bitcast.15) | data formatting | bytes 786432
Async XLA Ops:
  0.6 21.0 %copy-start = (s32[1,1,2,512]{3,2,1,0:T(2,128)S(1)}, s32[1,1,2,512]{3,2,1,0:T(2,128)}, u32[]{:S(2)}) copy-start(s32[1,1,2,512]{3,2,1,0:T(2,128)} %param.7) | copy-start | bytes 12292
  6.5 15.9 %collective-permute-start = (bf16[528,128]{1,0:T(8,128)(2,1)S(1)}, bf16[528,128]{1,0:T(8,128)(2,1)S(1)}, u32[]{:S(2)}, u32[]{:S(2)}) collective-permute-start(bf16[528,128]{1,0:T(8,128)(2,1)S(1)} %get-tuple-element.12), channel_id=1, source_target_pairs={{4,8},{12,16},{20,24},{28,32},{36,40},{44,48},{52,56},{60,64},{68,... | collective-permute-start | bytes 405512 | tf_op jit(solution)/shard_map/ppermute | solution.py:206
  19.7 3.2 %collective-permute-start.1 = (bf16[528,128]{1,0:T(8,128)(2,1)S(1)}, bf16[528,128]{1,0:T(8,128)(2,1)S(1)}, u32[]{:S(2)}, u32[]{:S(2)}) collective-permute-start(bf16[528,128]{1,0:T(8,128)(2,1)S(1)} %get-tuple-element.13), channel_id=1, source_target_pairs={{0,4},{4,0},{8,12},{12,8},{16,20},{20,16},{24,28},{28,24},{32,36},... | collective-permute-start | bytes 405512 | tf_op jit(solution)/shard_map/ppermute | solution.py:207
  21.7 1.3 %copy-start.1 = (f32[1,1,128]{2,1,0:T(1,128)S(1)}, f32[1,1,128]{2,1,0:T(1,128)}, u32[]{:S(2)}) copy-start(f32[1,1,128]{2,1,0:T(1,128)} %param.9) | copy-start | bytes 1540
  21.7 1.3 %copy-start.2 = (s32[1,1,16,1]{2,3,1,0:T(1,128)S(1)}, s32[1,1,16,1]{2,3,1,0:T(1,128)}, u32[]{:S(2)}) copy-start(s32[1,1,16,1]{2,3,1,0:T(1,128)} %param.8) | copy-start | bytes 196

commit v6 on v5

--- a/solution.py
+++ b/solution.py
@@ -161,7 +161,7 @@
     row_v[:, pl.ds(pl.multiple_of(2 * lanes - at, lanes), lanes)] = by_inner
     row_v[:, pl.ds(lanes, lanes)] = own
     total = by_cross * joined(cross) + own * vec[...] + by_inner * joined(inner)
-    product[...] = jnp.sum(total.T, axis=0, keepdims=True)
+    product[...] = jnp.sum(total, axis=1).reshape(1, -1)
     for q in range(tiles.shape[0]):
         used[q] = 0
     for t in range(owner.shape[1]):

time: 37.8 us -> 37.8 us (level)
  no operation moved by 1% of the time
where the time goes in v6:
time: 37.8 us; the launch traced here: 37.6 us
  starting transfers between devices  15.1 us (40%)
  blocking collectives  12.5 us (33%)
  Pallas kernels  7.89 us (21%)
  local copies, waits for them, and re-layouts  0.76 us (2%)
  between operations  0.7 us (2%)
  waiting for transfers between devices  0.63 us (2%)
    ppermute x1, starting transfers between devices, per_device(): got_cross = lax.ppermute(cross, 'sub', pairs + [(j, i) for i, j in pairs])  13.2 us
    all_to_all x1, blocking collectives, per_device(): received = lax.all_to_all(tiles, 'own', 0, 0, tiled=True)  12.5 us
    pallas_call x1, Pallas kernels, per_device(): pl.pallas_call(apply_kernel, name='apply', out_shape=(sent, sent, square,...  5.86 us
    ppermute x1, starting transfers between devices, per_device(): got_inner = lax.ppermute(inner, 'sub', [(i, i ^ 1) for i in range(chain)])  1.92 us
    pallas_call x1, Pallas kernels, per_device(): pl.pallas_call(pack_kernel, name='pack', out_shape=(jax.ShapeDtypeStruct(...  1.38 us
    unnamed x7, local copies, waits for them, and re-layouts  0.76 us
  transfers between devices with their start and end apart: 2, of which 2 were waited for; matrix products, arithmetic and copies ran while one was open for 0% of the time, Pallas kernels for 2%

profile of v6, /device:TPU:56, one launch (start us, length us, event | category | flops | bytes accessed | tf_op | source)
XLA Modules:
  0.0 37.6 jit_solution(9971083715476401607)
XLA Ops:
  0.6 0.0 copy-start
  0.6 5.9 %apply.1 = (bf16[528,128]{1,0:T(8,128)(2,1)S(1)}, bf16[528,128]{1,0:T(8,128)(2,1)S(1)}, f32[128,128]{1,0:T(8,128)S(1)}, bf16[8192,128]{1,0:T(8,128)(2,1)S(1)}, b...) custom-call(s32[2,512]{1,0:T(2,128)} %bitcast.9, bf16[8192,128]{1,0:T(8,128)(2,1)} %bitcast.14, ...), custom_call_target="tpu_custom_call" | custom-call | flops 536870912 | bytes 4194304 | tf_op jit(solution)/shard_map/apply/pallas_call | solution.py:188
  6.5 13.2 %collective-permute-start = (bf16[528,128]{1,0:T(8,128)(2,1)S(1)}, bf16[528,128]{1,0:T(8,128)(2,1)S(1)}, u32[]{:S(2)}, u32[]{:S(2)}) collective-permute-start(bf16[528,128]{1,0:T(8,128)(2,1)S(1)} %get-tuple-element.12), channel_id=1, source_target_pairs={{4,8},{12,16},{20,24},{28,32},{36,40},{44,48},{52,56},{60,64},{68,... | collective-permute-start | bytes 405512 | tf_op jit(solution)/shard_map/ppermute | solution.py:206
  19.7 1.9 %collective-permute-start.1 = (bf16[528,128]{1,0:T(8,128)(2,1)S(1)}, bf16[528,128]{1,0:T(8,128)(2,1)S(1)}, u32[]{:S(2)}, u32[]{:S(2)}) collective-permute-start(bf16[528,128]{1,0:T(8,128)(2,1)S(1)} %get-tuple-element.13), channel_id=1, source_target_pairs={{0,4},{4,0},{8,12},{12,8},{16,20},{20,16},{24,28},{28,24},{32,36},... | collective-permute-start | bytes 405512 | tf_op jit(solution)/shard_map/ppermute | solution.py:207
  21.6 0.0 copy-done
  21.7 0.0 copy-start.1
  21.7 0.0 copy-start.2
  21.7 0.7 %basis.1 = (bf16[128,1024]{1,0:T(8,128)(2,1)S(1)}, f32[128,128]{1,0:T(8,128)S(1)}) custom-call(s32[2,512]{1,0:T(2,128)S(1)} %bitcast.10, bf16[8192,128]{1,0:T(8,128)(2,1)S(1)} %get-tuple-element.14.z, bf16[8192,128]{1,0:T(8,128)(2,1)S(1)} %get-tuple-element.15.applied, bf16[128,1024]{1,0:T(8,128)(2,1)S(1)} %get-tuple-element.16.given, ...), custom_call_target="tpu_custom_call" | custom-call | flops 268435456 | bytes 2097152 | tf_op jit(solution)/shard_map/basis/pallas_call | solution.py:208
  22.3 0.1 collective-permute-done.cross
  22.4 0.6 %collective-permute-done.1.inner = bf16[528,128]{1,0:T(8,128)(2,1)S(1)} collective-permute-done((bf16[528,128]{1,0:T(8,128)(2,1)S(1)}, bf16[528,128]{1,0:T(8,128)(2,1)S(1)}, u32[]{:S(2)}, u32[]{:S(2)}) %collective-permute-start.1) | collective-permute-done | bytes 135200 | tf_op jit(solution)/shard_map/ppermute | solution.py:207
  23.0 0.0 copy-done.1
  23.0 0.0 copy-done.2
  23.0 1.4 %pack.1 = (f32[4,8,8,384]{3,2,1,0:T(8,128)S(1)}, f32[1,128]{1,0:T(1,128)}) custom-call(s32[1,16]{1,0:T(1,128)S(1)} %bitcast.13, bf16[528,128]{1,0:T(8,128)(2,1)S(1)} %collective-permute-done.cross, bf16[528,128]{1,0:T(8,128)(2,1)S(1)} %collective-permute-done.1.inner, bf16[128,1024]{1,0:T(8,128)(2,1)S(1)} %get-tuple-element.18.zt, ...), custom_call_target="tpu_custom_call" | custom-call | tf_op jit(solution)/shard_map/pack/pallas_call | solution.py:218
  24.3 12.5 %all_to_all.5 = f32[4,8,8,384]{3,2,1,0:T(8,128)S(1)} all-to-all(f32[4,8,8,384]{3,2,1,0:T(8,128)S(1)} %get-tuple-element.20), channel_id=1, replica_groups=mesh['sub'=192,'own'=4] {'own'}, dimensions={0} | all-to-all | bytes 786432 | tf_op jit(solution)/shard_map/all_to_all | solution.py:230
  36.8 0.7 %copy.8 = f32[1,1,4,8,8,384]{5,4,3,2,1,0:T(8,128)} copy(f32[1,1,4,8,8,384]{5,4,3,2,1,0:T(8,128)S(1)} %bitcast.15) | data formatting | bytes 786432
Async XLA Ops:
  0.6 21.0 %copy-start = (s32[1,1,2,512]{3,2,1,0:T(2,128)S(1)}, s32[1,1,2,512]{3,2,1,0:T(2,128)}, u32[]{:S(2)}) copy-start(s32[1,1,2,512]{3,2,1,0:T(2,128)} %param.7) | copy-start | bytes 12292
  6.5 15.9 %collective-permute-start = (bf16[528,128]{1,0:T(8,128)(2,1)S(1)}, bf16[528,128]{1,0:T(8,128)(2,1)S(1)}, u32[]{:S(2)}, u32[]{:S(2)}) collective-permute-start(bf16[528,128]{1,0:T(8,128)(2,1)S(1)} %get-tuple-element.12), channel_id=1, source_target_pairs={{4,8},{12,16},{20,24},{28,32},{36,40},{44,48},{52,56},{60,64},{68,... | collective-permute-start | bytes 405512 | tf_op jit(solution)/shard_map/ppermute | solution.py:206
  19.7 3.2 %collective-permute-start.1 = (bf16[528,128]{1,0:T(8,128)(2,1)S(1)}, bf16[528,128]{1,0:T(8,128)(2,1)S(1)}, u32[]{:S(2)}, u32[]{:S(2)}) collective-permute-start(bf16[528,128]{1,0:T(8,128)(2,1)S(1)} %get-tuple-element.13), channel_id=1, source_target_pairs={{0,4},{4,0},{8,12},{12,8},{16,20},{20,16},{24,28},{28,24},{32,36},... | collective-permute-start | bytes 405512 | tf_op jit(solution)/shard_map/ppermute | solution.py:207
  21.7 1.3 %copy-start.1 = (f32[1,1,128]{2,1,0:T(1,128)S(1)}, f32[1,1,128]{2,1,0:T(1,128)}, u32[]{:S(2)}) copy-start(f32[1,1,128]{2,1,0:T(1,128)} %param.9) | copy-start | bytes 1540
  21.7 1.3 %copy-start.2 = (s32[1,1,16,1]{2,3,1,0:T(1,128)S(1)}, s32[1,1,16,1]{2,3,1,0:T(1,128)}, u32[]{:S(2)}) copy-start(s32[1,1,16,1]{2,3,1,0:T(1,128)} %param.8) | copy-start | bytes 196
